TPU v7x, 32 devices: a whole 2x2x4 slice. The times are simulated.
32 devices in a mesh: dp: 8 (over z, y), tensor: 4 (over x, core).
Axes of the slice: x: 2, y: 2, z: 4, core: 2. Of those that a mesh axis runs over, the one named last changes fastest.
Arguments:
- hidden: bfloat16 [4096, 11008], P('dp', 'tensor'), may hold values from -6 to 6
- next_hidden: bfloat16 [4096, 11008], P('dp', 'tensor'), may hold values from -6 to 6
- out_grad: bfloat16 [4096, 4096], P('dp'), may hold values from -0.09375 to 0.09375
- sign_bits: int32 [16, 256], replicated, may hold values from 0 to 1
- scale_index: int32 [11008, 16], P('tensor'), may hold values from 0 to 3
- master: float32 [11008, 4096], P(('tensor', 'dp')), may hold values from -0.0546875 to 0.0546875
- moment_one: float32 [11008, 4096], P(('tensor', 'dp')), may hold values from -1.5 to 1.5
- moment_two: float32 [11008, 4096], P(('tensor', 'dp')), may hold values from 0.01 to 1
Outputs:
- gradient: float32 [11008, 4096], P(('tensor', 'dp'))
- new_master: float32 [11008, 4096], P(('tensor', 'dp'))
- new_moment_one: float32 [11008, 4096], P(('tensor', 'dp'))
- new_moment_two: float32 [11008, 4096], P(('tensor', 'dp'))
- next_out: bfloat16 [4096, 4096], P(('dp', 'tensor'))
All inputs are finite; a program needn't handle non-finite values.
Results may differ from a plain program's by a relative error of at most 0.023.
Values may be sent and summed in bfloat16 or wider, within the bound.
No kernel may reach another device: no remote copies, remote signals or barrier semaphores. Data moves between devices by JAX's collectives and lax.ppermute only.
A program may use at most 192 MiB of HBM per device.

v0:
```python
import math

import jax
import jax.numpy as jnp
import numpy as np
from jax import lax
from jax.experimental import pallas as pl
from jax.experimental.pallas import tpu as pltpu
from jax.sharding import PartitionSpec as P

BLOCK = 256


CLIP_LEVEL = 127.0
LEARN_RATE = 0.005
BETA_ONE = 0.9
BETA_TWO = 0.95
WEIGHT_DECAY = 0.1
EPSILON = 1e-08
FIRST_BIAS = 1.0 - (0.9**50) ** 2
SECOND_BIAS = 1.0 - (0.95**50) ** 2
LEVELS = (16.0, 32.0, 64.0, 128.0)
CHUNKS = 4
GROUPS = 4
ADAM_STEPS = 2
FORWARD_STEPS = 2
ORDER = (
    "rot",
    "tu0",
    "g10",
    "tu3",
    "g11",
    "tu2",
    "g12",
    "ay0",
    "g13",
    "ay1",
    "ad0",
    "tu1",
    "ay2",
    "ad1",
    "g20",
    "ay3",
    "ad2",
    "g21",
    "sc0",
    "ad3",
    "g22",
    "sc1",
    "sx0",
    "g23",
    "sc2",
    "sx1",
    "sn0",
    "sc3",
    "sx2",
    "sn1",
    "sx3",
    "sn2",
    "sn3",
)
COST = {"ro": 300000000, "st": 25000000000, "ay": 300000000, "g1": 300000000, "ad": 300000000, "tu": 300000000, "g2": 300000000, "sc": 300000000, "sx": 300000000, "sn": 300000000}
VMEM_BYTES = 28 * 1024 * 1024


def hadamard(block_size):
    positions = np.arange(block_size)
    common_bits = positions[:, None] & positions[None, :]
    parity = np.zeros((block_size, block_size), np.int32)
    for bit_shift in range(block_size.bit_length() - 1):
        parity += (common_bits >> bit_shift) & 1
    return ((1 - 2 * (parity & 1)) / math.sqrt(block_size)).astype(np.float32)


def dot(a, b):
    return lax.dot_general(a, b, (((1,), (0,)), ((), ())), preferred_element_type=jnp.float32)


def block_spec(shape, index_map):
    return pl.BlockSpec(shape, index_map)


def whole(shape):
    return pl.BlockSpec(shape, lambda i, p: (0,) * len(shape))


class Chain:
    def __init__(self, place):
        self.place = place
        self.held = []

    def note(self, value):
        self.held.append(value)

    def __call__(self, name, body, grid, in_specs, out_specs, out_shape, scratch, args, aliases=None, token=0):
        held = self.held
        count, extra = len(args), len(held)

        def wrapped(place_ref, *refs):
            body(place_ref, *refs[:count], *refs[count + extra :])

        outs = pl.pallas_call(
            wrapped,
            grid_spec=pltpu.PrefetchScalarGridSpec(
                num_scalar_prefetch=1,
                grid=grid,
                in_specs=list(in_specs) + [pl.BlockSpec(memory_space=pl.ANY)] * extra,
                out_specs=out_specs,
                scratch_shapes=scratch,
            ),
            out_shape=out_shape,
            input_output_aliases=aliases or {},
            compiler_params=pltpu.CompilerParams(vmem_limit_bytes=VMEM_BYTES),
            cost_estimate=pl.CostEstimate(flops=COST[name[:2]], bytes_accessed=1000, transcendentals=0),
        )(self.place, *args, *held)
        self.held = [outs[token]]
        return outs


def rotate(chain, out_grad, flips, matrix):
    rows, width = out_grad.shape
    step = width // CHUNKS
    piece = step // 4
    per_group = CHUNKS // GROUPS

    def body(place_ref, grad_ref, flips_ref, matrix_ref, out_ref, *own_refs):
        position = place_ref[0]
        for block in range(step // BLOCK):
            columns = slice(block * BLOCK, (block + 1) * BLOCK)
            signed = grad_ref[:, columns] * flips_ref[block]
            out_ref[:, columns] = dot(signed, matrix_ref[...]).astype(jnp.bfloat16)
        for chunk in range(CHUNKS):

            @pl.when(pl.program_id(0) == chunk)
            def _():
                start = (chunk % per_group) * piece
                own = out_ref[:, pl.ds(pl.multiple_of(position * piece, BLOCK), piece)]
                own_refs[chunk // per_group][:, start : start + piece] = own

    return chain(
        "rot",
        body,
        (CHUNKS,),
        [
            block_spec((rows, step), lambda b, p: (0, b)),
            block_spec((step // BLOCK, 1, BLOCK), lambda b, p: (b, 0, 0)),
            whole((BLOCK, BLOCK)),
        ],
        [block_spec((rows, step), lambda b, p: (0, b))] + [whole((rows, per_group * piece))] * GROUPS,
        [jax.ShapeDtypeStruct((rows, width), jnp.bfloat16)]
        + [jax.ShapeDtypeStruct((rows, per_group * piece), jnp.bfloat16)] * GROUPS,
        [],
        (out_grad, flips.reshape(width // BLOCK, 1, BLOCK), matrix),
    )


def coded_sum(chain, chunk, hidden_parts, rotated, pieces, scales):
    units, tokens = hidden_parts[1].shape
    rows = units // 2
    width = rotated.shape[1] // CHUNKS
    piece = width // 4
    block_count = scales.shape[1]

    def body(place_ref, own_hidden, near_hidden, far_hidden, own_ref, u_ref, cu_ref, v_ref, cv_ref, scales_ref, keep_ref, send_ref, acc_ref):
        position, y = place_ref[0], place_ref[1]
        mine = pl.ds(pl.multiple_of(y * rows, 8), rows)
        theirs = pl.ds(pl.multiple_of((1 - y) * rows, 8), rows)
        lane = lax.broadcasted_iota(jnp.int32, (2 * rows, block_count), 1)
        all_scales = scales_ref[...]
        received = jnp.where(pl.program_id(0) == 0, near_hidden[...], far_hidden[...])
        for j, ref in enumerate((u_ref, cu_ref, v_ref, cv_ref)):
            quarter = jnp.bitwise_xor(position, j)
            for part in range(piece // BLOCK):
                column = pl.multiple_of(quarter * piece + part * BLOCK, BLOCK)
                columns = pl.ds(column, BLOCK)
                block = chunk * (width // BLOCK) + quarter * (piece // BLOCK) + part
                scale = jnp.sum(jnp.where(lane == block, all_scales, 0.0), axis=1, keepdims=True)

                def coded(hidden, values):
                    product = dot(hidden, values) * scale
                    return jnp.clip(product, -CLIP_LEVEL, CLIP_LEVEL).astype(jnp.bfloat16).astype(jnp.float32)

                values, other = own_ref[:, columns], ref[:, part * BLOCK : (part + 1) * BLOCK]

                acc_ref[...] = coded(own_hidden[...], values) + coded(received, other)
                keep_ref[0, :, columns] = acc_ref[mine, :].astype(jnp.bfloat16)
                send_ref[0, :, columns] = acc_ref[theirs, :].astype(jnp.bfloat16)

    out = jax.ShapeDtypeStruct((2, rows, width), jnp.bfloat16)
    part_spec = block_spec((tokens, piece), lambda i, p: (0, chunk % (CHUNKS // GROUPS)))
    return chain(
        f"g1{chunk}",
        body,
        (2,),
        [block_spec((units, tokens), lambda i, p: (i, 0))]
        + [whole((units, tokens))] * 2
        + [block_spec((tokens, width), lambda i, p: (0, chunk))]
        + [part_spec] * 4
        + [block_spec((2 * rows, block_count), lambda i, p: (i, 0))],
        [block_spec((1, rows, width), lambda i, p: (jnp.bitwise_xor(i, p[2]), 0, 0))] * 2,
        [out, out],
        [pltpu.VMEM((2 * rows, BLOCK), jnp.float32)],
        (*hidden_parts, rotated, *pieces, scales),
    )


def adam(chain, chunk, kept, received, shard_scales, flips, matrix, master, one, two, previous):
    rows, width = kept.shape
    model_width = master.shape[1]
    block_count = shard_scales.shape[1]
    step = width // ADAM_STEPS
    parts = step // BLOCK
    chained = previous is not None

    def body(place_ref, kept_ref, received_ref, scales_ref, flips_ref, matrix_ref, master_ref, one_ref, two_ref, *rest):
        grad_out, master_out, one_out, two_out, weight_out = rest[-5:]
        lane = lax.broadcasted_iota(jnp.int32, (rows, block_count), 1)
        all_scales = scales_ref[...]
        for part in range(parts):
            block = (chunk * ADAM_STEPS + pl.program_id(0)) * parts + part
            columns = slice(part * BLOCK, (part + 1) * BLOCK)
            scale = jnp.sum(jnp.where(lane == block, all_scales, 0.0), axis=1, keepdims=True)
            decoded = dot(kept_ref[:, columns], matrix_ref[...]) + dot(received_ref[:, columns], matrix_ref[...])
            gradient = decoded / scale * flips_ref[part]
            new_one = BETA_ONE * one_ref[:, columns] + (1.0 - BETA_ONE) * gradient
            new_two = BETA_TWO * two_ref[:, columns] + (1.0 - BETA_TWO) * gradient * gradient
            update = new_one / FIRST_BIAS / (jnp.sqrt(new_two / SECOND_BIAS) + EPSILON)
            old = master_ref[:, columns]
            new_master = old - LEARN_RATE * (update + WEIGHT_DECAY * old)
            grad_out[:, columns] = gradient
            master_out[:, columns] = new_master
            one_out[:, columns] = new_one
            two_out[:, columns] = new_two
            weight_out[:, columns] = new_master.astype(jnp.bfloat16)

    local = block_spec((rows, step), lambda j, p: (0, j))
    placed = block_spec((rows, step), lambda j, p: (0, chunk * ADAM_STEPS + j))
    state = jax.ShapeDtypeStruct((rows, model_width), jnp.float32)
    return chain(
        f"ad{chunk}",
        body,
        (ADAM_STEPS,),
        [
            local,
            local,
            whole((rows, block_count)),
            block_spec((parts, 1, BLOCK), lambda j, p: (chunk * ADAM_STEPS + j, 0, 0)),
            whole((BLOCK, BLOCK)),
            placed,
            placed,
            placed,
        ]
        + ([pl.BlockSpec(memory_space=pl.ANY)] * 4 if chained else []),
        [placed] * 4 + [local],
        [state] * 4 + [jax.ShapeDtypeStruct((rows, width), jnp.bfloat16)],
        [],
        (
            kept,
            received,
            shard_scales,
            flips.astype(jnp.float32).reshape(block_count, 1, BLOCK),
            matrix,
            *(pltpu.with_memory_space_constraint(value, pltpu.HBM) for value in (master, one, two)),
            *(previous if chained else ()),
        ),
        {9 + i: i for i in range(4)} if chained else None,
        token=4,
    )


def forward(chain, name, inputs, weight, other):
    tokens, units = inputs[0].shape
    rows, width = weight.shape
    quarter = tokens // 4
    step = width // FORWARD_STEPS

    def body(place_ref, n0, n1, n2, n3, weight_ref, other_ref, o0, o1, o2, o3, acc_ref, joined_ref):
        position, y = place_ref[0], place_ref[1]
        joined_ref[pl.ds(pl.multiple_of(y * rows, 8), rows), :] = weight_ref[...].astype(jnp.float32)
        joined_ref[pl.ds(pl.multiple_of((1 - y) * rows, 8), rows), :] = other_ref[...].astype(jnp.float32)
        joined = joined_ref[...].astype(jnp.bfloat16)
        for k, ref in enumerate((n0, n2, n1, n3)):
            acc_ref[...] = dot(ref[...], joined).astype(jnp.bfloat16)
            for i, out_ref in enumerate((o0, o1, o2, o3)):
                start = jnp.bitwise_xor(position, i) * quarter
                out_ref[k] = acc_ref[pl.ds(pl.multiple_of(start, quarter), quarter), :]

    return chain(
        name,
        body,
        (FORWARD_STEPS,),
        [whole((tokens, units))] * 4 + [block_spec((rows, step), lambda j, p: (0, j))] * 2,
        [block_spec((4, quarter, step), lambda j, p: (0, 0, j))] * 4,
        [jax.ShapeDtypeStruct((4, quarter, width), jnp.bfloat16)] * 4,
        [pltpu.VMEM((tokens, step), jnp.bfloat16), pltpu.VMEM((units, step), jnp.float32)],
        (*inputs, weight, other),
    )


def add(a, b):
    return (a.astype(jnp.float32) + b.astype(jnp.float32)).astype(jnp.bfloat16)


def on_device(
    hidden, next_hidden, out_grad, sign_bits, scale_index, master, moment_one, moment_two
):
    dp_size = lax.axis_size("dp")
    tensor_size = lax.axis_size("tensor")
    tokens = hidden.shape[0]
    shard_rows = master.shape[0]
    block_count = sign_bits.shape[0]
    replica = lax.axis_index("dp")
    group = lax.axis_index("tensor")
    z, y = replica // 2, replica % 2
    far_side = replica // 4
    place = jnp.stack([group, y, far_side]).astype(jnp.int32)
    matrix = jnp.asarray(hadamard(BLOCK)).astype(jnp.bfloat16)
    flips = (1 - 2 * sign_bits).astype(jnp.bfloat16)

    def over_dp(value, bits):
        return lax.ppermute(value, "dp", [(i, i ^ bits) for i in range(dp_size)])

    def over_tensor(value, bits):
        return lax.ppermute(value, "tensor", [(i, i ^ bits) for i in range(tensor_size)])

    units = 2 * shard_rows
    near_z = z % 2
    by_pair = hidden.T.reshape(2, 2, units, tokens)

    def pair_rows(values, k):
        picked = lax.dynamic_index_in_dim(values, near_z ^ k, 1, keepdims=False)
        return picked.reshape(2 * units, picked.shape[-1])

    hidden_parts = [pair_rows(by_pair, 0)] + [
        over_dp(lax.dynamic_index_in_dim(half, 1 - near_z, 0, keepdims=False), 2) for half in by_pair
    ]
    chain = Chain(place)
    rotated, *own_pieces = rotate(chain, out_grad, flips, matrix)

    level_table = jnp.array(LEVELS, jnp.float32)
    matches = (scale_index[:, :, None] == jnp.arange(4, dtype=jnp.int32)).astype(jnp.float32)
    all_scales = jnp.sum(matches * level_table, axis=-1) * math.sqrt(dp_size)
    scales = pair_rows(all_scales.reshape(2, 2, units, block_count), 0)
    shard_scales = lax.dynamic_slice_in_dim(scales, (2 * far_side + y) * shard_rows, shard_rows, 0)

    next_t = next_hidden.T
    inputs = [lax.dynamic_slice_in_dim(next_t, (z ^ k) * units, units, 0) for k in range(4)]
    inputs = [inputs[0]] + [over_dp(inputs[k], 2 * k) for k in range(1, 4)]

    state = None
    pieces, kept, halves, arriving, weights, partials, sums, nears, outs = ({} for _ in range(9))
    turned_inputs = {}

    def gather(k):
        u = over_dp(own_pieces[k], 2)
        v = over_tensor(u, 2)
        pieces[k] = (u, over_tensor(u, 1), v, over_tensor(v, 1))

    def first(k):
        kept[k], sent = coded_sum(chain, k, hidden_parts, rotated, pieces[k // (CHUNKS // GROUPS)], scales)
        halves[k] = over_dp(sent, 1)

    def join_rows(k):
        go = add(kept[k][1], halves[k][1])
        kept[k] = add(kept[k][0], halves[k][0])
        arriving[k] = over_dp(go, 4)
        chain.note(go)

    def update(k):
        nonlocal state
        *state, weight = adam(
            chain, k, kept[k], arriving[k], shard_scales, flips, matrix, master, moment_one, moment_two, state
        )
        weights[k] = (weight, over_dp(weight, 1))

    def turn(k):
        turned_inputs[k] = inputs[k].T
        chain.note(inputs[k])

    def second(k):
        stay, near, go, far = forward(chain, f"g2{k}", [turned_inputs[i] for i in range(4)], *weights[k])
        partials[k] = (stay, go, over_tensor(near, 1), over_tensor(far, 1))

    def sum_cores(k):
        stay, go, near, far = partials[k]
        go = add(go, far)
        sums[k] = (add(stay, near), over_tensor(go, 2))
        chain.note(go)

    def sum_chips(k):
        stay, more = sums[k]
        go = add(stay[2:], more[2:])
        nears[k] = (add(stay[:2], more[:2]), over_dp(go, 2))
        chain.note(go)

    def sum_near(k):
        stay, more = nears[k]
        go = add(stay[1], more[1])
        outs[k] = (add(stay[0], more[0]), over_dp(go, 4))
        chain.note(go)

    steps = {"tu": turn, "ay": join_rows, "g1": first, "ad": update, "g2": second, "sc": sum_cores, "sx": sum_chips, "sn": sum_near}
    for group_index in range(GROUPS):
        gather(group_index)
    for name in ORDER[1:]:
        steps[name[:2]](int(name[2:]))
    next_out = jnp.concatenate([add(*outs[k]) for k in range(CHUNKS)], axis=1)
    gradient, new_master, new_one, new_two = state
    return (gradient, new_master, new_one, new_two, next_out)


def general(
    hidden, next_hidden, out_grad, sign_bits, scale_index, master, moment_one, moment_two
):
    dp_size = lax.axis_size("dp")
    tok_rows = hidden.shape[0]
    model_width = out_grad.shape[1]
    block_count = sign_bits.shape[0]
    shard_rows = master.shape[0]
    matrix = jnp.asarray(hadamard(BLOCK))
    sign_flips = (1 - 2 * sign_bits).astype(jnp.float32)
    signed = out_grad.reshape(tok_rows, block_count, BLOCK) * sign_flips.astype(jnp.bfloat16)
    rotated = jnp.einsum(
        "tbj,jk->tbk", signed, matrix.astype(jnp.bfloat16), preferred_element_type=jnp.float32
    )
    rotated = rotated.astype(jnp.bfloat16).reshape(tok_rows, model_width)
    level_table = jnp.array(LEVELS, jnp.float32)
    matches = (scale_index[:, :, None] == jnp.arange(4, dtype=jnp.int32)).astype(jnp.float32)
    scales = jnp.sum(matches * level_table, axis=-1) * math.sqrt(dp_size)
    product = lax.dot_general(
        hidden, rotated, (((0,), (0,)), ((), ())), preferred_element_type=jnp.float32
    )
    scaled = product.reshape(dp_size * shard_rows, block_count, BLOCK) * scales[:, :, None]
    summed = lax.psum_scatter(
        jnp.clip(scaled, -CLIP_LEVEL, CLIP_LEVEL)
        .reshape(dp_size * shard_rows, model_width)
        .astype(jnp.bfloat16),
        "dp",
        scatter_dimension=0,
        tiled=True,
    ).astype(jnp.float32)
    shard_scales = lax.dynamic_slice_in_dim(
        scales, lax.axis_index("dp") * shard_rows, shard_rows, 0
    )
    unscaled = summed.reshape(shard_rows, block_count, BLOCK) / shard_scales[:, :, None]
    decoded = jnp.einsum("rbj,jk->rbk", unscaled, matrix, precision=lax.Precision.HIGHEST)
    gradient = (decoded * sign_flips).reshape(shard_rows, model_width)
    new_one = BETA_ONE * moment_one + (1.0 - BETA_ONE) * gradient
    new_two = BETA_TWO * moment_two + (1.0 - BETA_TWO) * gradient * gradient
    update = new_one / FIRST_BIAS / (jnp.sqrt(new_two / SECOND_BIAS) + EPSILON)
    new_master = master - LEARN_RATE * (update + WEIGHT_DECAY * master)
    partial_value = jnp.dot(
        next_hidden,
        lax.all_gather(new_master.astype(jnp.bfloat16), "dp", axis=0, tiled=True),
        preferred_element_type=jnp.float32,
    )
    next_out = lax.psum_scatter(
        partial_value.astype(jnp.bfloat16), "tensor", scatter_dimension=0, tiled=True
    )
    return (gradient, new_master, new_one, new_two, next_out)


def solution(mesh):
    grouped = mesh.shape["dp"] == 8 and mesh.shape["tensor"] == 4
    return jax.shard_map(
        on_device if grouped else general,
        mesh=mesh,
        in_specs=(
            P("dp", "tensor"),
            P("dp", "tensor"),
            P("dp", None),
            P(),
            P("tensor", None),
            P(("tensor", "dp"), None),
            P(("tensor", "dp"), None),
            P(("tensor", "dp"), None),
        ),
        out_specs=(
            P(("tensor", "dp"), None),
            P(("tensor", "dp"), None),
            P(("tensor", "dp"), None),
            P(("tensor", "dp"), None),
            P(("dp", "tensor"), None),
        ),
        check_vma=False,
    )
```

profile of v0, /device:TPU:0, one launch (start us, length us, event | category | flops | bytes accessed | tf_op | source)
XLA Modules:
  0.0 380.4 jit_solution(11904620477099792657)
XLA Ops:
  1.5 2.2 copy-done.13
  4.6 3.8 shard_map.137
  8.4 2.0 copy-done
  11.8 3.0 collective-permute-start.14
  14.8 2.0 fusion.21
  18.6 2.0 collective-permute-start.1
  22.0 2.0 collective-permute-start.16
  24.8 4.2 %collective-permute-done.16.refs_6_ = bf16[512,256]{1,0:T(8,128)(2,1)} collective-permute-done((bf16[512,256]{1,0:T(8,128)(2,1)}, bf16[512,256]{1,0:T(8,128)(2,1)}, u32[]{:S(2)}, u32[]{:S(2)}) %collective-permute-start.16) | collective-permute-done | bytes 262176 | tf_op jit(solution)/shard_map/ppermute | solution.py:324
  29.0 2.9 dynamic-slice_bitcast_fusion
  32.1 3.9 %collective-permute-start.18 = (bf16[688,512]{1,0:T(8,128)(2,1)S(1)}, bf16[688,512]{1,0:T(8,128)(2,1)S(1)}, u32[]{:S(2)}, u32[]{:S(2)}) collective-permute-start(bf16[688,512]{1,0:T(8,128)(2,1)S(1)} %get-tuple-element.104), channel_id=1, source_target_pairs={{0,24},{4,28},{8,16},{12,20},{16,8},{20,12},{24,0},{28,4},{1,25},{... | collective-permute-start | bytes 2113544 | tf_op jit(solution)/shard_map/ppermute | solution.py:321
  37.0 15.1 %collective-permute-done.1.refs_2_ = bf16[688,512]{1,0:T(8,128)(2,1)S(1)} collective-permute-done((bf16[688,512]{1,0:T(8,128)(2,1)}, bf16[688,512]{1,0:T(8,128)(2,1)S(1)}, u32[]{:S(2)}, u32[]{:S(2)}) %collective-permute-start.1) | collective-permute-done | bytes 704544 | tf_op jit(solution)/shard_map/ppermute | solution.py:321
  52.1 5.4 %shard_map.138 = (bf16[2,344,1024]{2,1,0:T(8,128)(2,1)S(1)}, bf16[2,344,1024]{2,1,0:T(8,128)(2,1)S(1)}) custom-call(s32[3]{0:T(128)S(1)} %pad_add_fusion.place_ref, bf16[1376,512]{1,0:T(8,128)(2,1)S(1)} %bitcast.75, bf16[688,512]{1,0:T(8,128)(2,1)S(1)} %collective-permute-done.refs_1_, bf16[688,512]{1,0:T(8,128)(2,1)S(1)} %collective-permute-done.1.refs_2_, ...), custom_call_target="tpu_custom_call" | custom-call | flops 300000000 | bytes 1000 | tf_op jit(solution)/shard_map/pallas_call | solution.py:102
  57.5 2.1 collective-permute-start.20
  61.1 5.1 %collective-permute-done.12.refs_6_ = bf16[512,256]{1,0:T(8,128)(2,1)S(1)} collective-permute-done((bf16[512,256]{1,0:T(8,128)(2,1)}, bf16[512,256]{1,0:T(8,128)(2,1)S(1)}, u32[]{:S(2)}, u32[]{:S(2)}) %collective-permute-start.12) | collective-permute-done | bytes 262176 | tf_op jit(solution)/shard_map/ppermute | solution.py:324
  67.8 14.3 %collective-permute-start.19 = (bf16[688,512]{1,0:T(8,128)(2,1)S(1)}, bf16[688,512]{1,0:T(8,128)(2,1)S(1)}, u32[]{:S(2)}, u32[]{:S(2)}) collective-permute-start(bf16[688,512]{1,0:T(8,128)(2,1)S(1)} %get-tuple-element.106), channel_id=1, source_target_pairs={{0,16},{4,20},{8,24},{12,28},{16,0},{20,4},{24,8},{28,12},{1,17},{... | collective-permute-start | bytes 2113544 | tf_op jit(solution)/shard_map/ppermute | solution.py:321
  82.1 6.1 %shard_map.139 = (bf16[2,344,1024]{2,1,0:T(8,128)(2,1)S(1)}, bf16[2,344,1024]{2,1,0:T(8,128)(2,1)}) custom-call(s32[3]{0:T(128)S(1)} %pad_add_fusion.place_ref, bf16[1376,512]{1,0:T(8,128)(2,1)S(1)} %bitcast.76, bf16[688,512]{1,0:T(8,128)(2,1)S(1)} %collective-permute-done.refs_1_, bf16[688,512]{1,0:T(8,128)(2,1)S(1)} %collective-permute-done.1.refs_2_, ...), custom_call_target="tpu_custom_call" | custom-call | flops 300000000 | bytes 1000 | tf_op jit(solution)/shard_map/pallas_call | solution.py:102
  91.3 6.4 %collective-permute-done.8.refs_6_ = bf16[512,256]{1,0:T(8,128)(2,1)S(1)} collective-permute-done((bf16[512,256]{1,0:T(8,128)(2,1)S(1)}, bf16[512,256]{1,0:T(8,128)(2,1)S(1)}, u32[]{:S(2)}, u32[]{:S(2)}) %collective-permute-start.8) | collective-permute-done | bytes 262176 | tf_op jit(solution)/shard_map/ppermute | solution.py:324
  98.1 15.4 %collective-permute-done.19.refs_10_ = bf16[688,512]{1,0:T(8,128)(2,1)S(1)} collective-permute-done((bf16[688,512]{1,0:T(8,128)(2,1)S(1)}, bf16[688,512]{1,0:T(8,128)(2,1)S(1)}, u32[]{:S(2)}, u32[]{:S(2)}) %collective-permute-start.19) | collective-permute-done | bytes 704544 | tf_op jit(solution)/shard_map/ppermute | solution.py:321
  113.5 5.2 %shard_map.140 = (bf16[2,344,1024]{2,1,0:T(8,128)(2,1)S(1)}, bf16[2,344,1024]{2,1,0:T(8,128)(2,1)}) custom-call(s32[3]{0:T(128)S(1)} %pad_add_fusion.place_ref, bf16[1376,512]{1,0:T(8,128)(2,1)S(1)} %bitcast.77, bf16[688,512]{1,0:T(8,128)(2,1)S(1)} %collective-permute-done.refs_1_, bf16[688,512]{1,0:T(8,128)(2,1)S(1)} %collective-permute-done.1.refs_2_, ...), custom_call_target="tpu_custom_call" | custom-call | flops 300000000 | bytes 1000 | tf_op jit(solution)/shard_map/pallas_call | solution.py:102
  123.5 4.6 %collective-permute-done.4.refs_6_ = bf16[512,256]{1,0:T(8,128)(2,1)} collective-permute-done((bf16[512,256]{1,0:T(8,128)(2,1)}, bf16[512,256]{1,0:T(8,128)(2,1)}, u32[]{:S(2)}, u32[]{:S(2)}) %collective-permute-start.4) | collective-permute-done | bytes 262176 | tf_op jit(solution)/shard_map/ppermute | solution.py:324
  130.0 2.2 copy-done.2
  133.6 6.4 %shard_map.141 = (bf16[2,344,1024]{2,1,0:T(8,128)(2,1)S(1)}, bf16[2,344,1024]{2,1,0:T(8,128)(2,1)}) custom-call(s32[3]{0:T(128)S(1)} %pad_add_fusion.place_ref, bf16[1376,512]{1,0:T(8,128)(2,1)S(1)} %bitcast.78, bf16[688,512]{1,0:T(8,128)(2,1)S(1)} %collective-permute-done.refs_1_, bf16[688,512]{1,0:T(8,128)(2,1)S(1)} %collective-permute-done.1.refs_2_, ...), custom_call_target="tpu_custom_call" | custom-call | flops 300000000 | bytes 1000 | tf_op jit(solution)/shard_map/pallas_call | solution.py:102
  140.5 3.0 fusion.6
  145.2 13.1 %collective-permute-done.27.refs_1_ = bf16[344,1024]{1,0:T(8,128)(2,1)} collective-permute-done((bf16[344,1024]{1,0:T(8,128)(2,1)}, bf16[344,1024]{1,0:T(8,128)(2,1)}, u32[]{:S(2)}, u32[]{:S(2)}) %collective-permute-start.27) | collective-permute-done | bytes 704544 | tf_op jit(solution)/shard_map/ppermute | solution.py:321
  158.3 5.8 %shard_map.142 = (f32[344,4096]{1,0:T(8,128)}, f32[344,4096]{1,0:T(8,128)}, f32[344,4096]{1,0:T(8,128)}, f32[344,4096]{1,0:T(8,128)}, bf16[344,1024]{1,0:T(8,128)(2,1)}) custom-call(s32[3]{0:T(128)S(1)} %pad_add_fusion.place_ref, bf16[344,1024]{1,0:T(8,128)(2,1)S(1)} %copy-done.21, bf16[344,1024]{1,0:T(8,128)(2,1)} %collective-permute-done.27.refs_1_, ...), custom_call_target="tpu_custom_call" | custom-call | flops 300000000 | bytes 1000 | tf_op jit(solution)/shard_map/pallas_call | solution.py:102
  164.1 14.6 %collective-permute-start.29 = (bf16[344,1024]{1,0:T(8,128)(2,1)}, bf16[344,1024]{1,0:T(8,128)(2,1)}, u32[]{:S(2)}, u32[]{:S(2)}) collective-permute-start(bf16[344,1024]{1,0:T(8,128)(2,1)} %get-tuple-element.71.refs_12_.refs_4_), channel_id=1, source_target_pairs={{0,4},{4,0},{8,12},{12,8},{16,20},{20,16},{24,28},{28,24},{1,5},{5... | collective-permute-start | bytes 2113544 | tf_op jit(solution)/shard_map/ppermute | solution.py:321
  180.9 2.4 fusion.4
  183.4 18.4 %collective-permute-done.26.refs_1_ = bf16[344,1024]{1,0:T(8,128)(2,1)} collective-permute-done((bf16[344,1024]{1,0:T(8,128)(2,1)}, bf16[344,1024]{1,0:T(8,128)(2,1)}, u32[]{:S(2)}, u32[]{:S(2)}) %collective-permute-start.26) | collective-permute-done | bytes 704544 | tf_op jit(solution)/shard_map/ppermute | solution.py:321
  201.9 5.6 %shard_map.143 = (f32[344,4096]{1,0:T(8,128)}, f32[344,4096]{1,0:T(8,128)}, f32[344,4096]{1,0:T(8,128)}, f32[344,4096]{1,0:T(8,128)}, bf16[344,1024]{1,0:T(8,128)(2,1)S(1)}) custom-call(s32[3]{0:T(128)S(1)} %pad_add_fusion.place_ref, bf16[344,1024]{1,0:T(8,128)(2,1)S(1)} %copy-done.16, ...), custom_call_target="tpu_custom_call", output_to_operand_aliasing={{0}: (9, {}), {1}: (10, {}), {2}: (11, {}), {3}: (12, {})} | custom-call | flops 300000000 | bytes 1000 | tf_op jit(solution)/shard_map/pallas_call | solution.py:102
  208.6 6.0 %shard_map.144 = (bf16[4,128,1024]{2,1,0:T(8,128)(2,1)S(1)}, bf16[4,128,1024]{2,1,0:T(8,128)(2,1)S(1)}, bf16[4,128,1024]{2,1,0:T(8,128)(2,1)S(1)}, bf16[4,128,1024]{2,1,0:T(8,128)(2,1)S(1)}) custom-call(s32[3]{0:T(128)S(1)} %pad_add_fusion.place_ref, bf16[512,688]{1,0:T(8,128)(2,1)S(1)} %copy.70.refs_0_, bf16[512,688]{1,0:T(8,128)(2,1)S(1)} %bitcast.87, ...), custom_call_target="tpu_custom_call" | custom-call | flops 300000000 | bytes 1000 | tf_op jit(solution)/shard_map/pallas_call | solution.py:102
  216.7 5.5 %shard_map.145 = (f32[344,4096]{1,0:T(8,128)}, f32[344,4096]{1,0:T(8,128)}, f32[344,4096]{1,0:T(8,128)}, f32[344,4096]{1,0:T(8,128)}, bf16[344,1024]{1,0:T(8,128)(2,1)S(1)}) custom-call(s32[3]{0:T(128)S(1)} %pad_add_fusion.place_ref, ...), custom_call_target="tpu_custom_call", output_to_operand_aliasing={{0}: (9, {}), {1}: (10, {}), {2}: (11, {}), {3}: (12, {})} | custom-call | flops 300000000 | bytes 1000 | tf_op jit(solution)/shard_map/pallas_call | solution.py:102
  222.3 2.8 collective-permute-done.30.refs_5_
  225.1 5.0 %shard_map.146 = (bf16[4,128,1024]{2,1,0:T(8,128)(2,1)S(1)}, bf16[4,128,1024]{2,1,0:T(8,128)(2,1)S(1)}, bf16[4,128,1024]{2,1,0:T(8,128)(2,1)S(1)}, bf16[4,128,1024]{2,1,0:T(8,128)(2,1)S(1)}) custom-call(s32[3]{0:T(128)S(1)} %pad_add_fusion.place_ref, bf16[512,688]{1,0:T(8,128)(2,1)S(1)} %copy.70.refs_0_, bf16[512,688]{1,0:T(8,128)(2,1)S(1)} %bitcast.88, ...), custom_call_target="tpu_custom_call" | custom-call | flops 300000000 | bytes 1000 | tf_op jit(solution)/shard_map/pallas_call | solution.py:102
  231.9 31.1 %collective-permute-done.22.refs_1_ = bf16[344,1024]{1,0:T(8,128)(2,1)S(1)} collective-permute-done((bf16[344,1024]{1,0:T(8,128)(2,1)S(1)}, bf16[344,1024]{1,0:T(8,128)(2,1)S(1)}, u32[]{:S(2)}, u32[]{:S(2)}) %collective-permute-start.22) | collective-permute-done | bytes 704544 | tf_op jit(solution)/shard_map/ppermute | solution.py:321
  263.1 5.5 %shard_map.147 = (f32[344,4096]{1,0:T(8,128)}, f32[344,4096]{1,0:T(8,128)}, f32[344,4096]{1,0:T(8,128)}, f32[344,4096]{1,0:T(8,128)}, bf16[344,1024]{1,0:T(8,128)(2,1)S(1)}) custom-call(s32[3]{0:T(128)S(1)} %pad_add_fusion.place_ref, ...), custom_call_target="tpu_custom_call", output_to_operand_aliasing={{0}: (9, {}), {1}: (10, {}), {2}: (11, {}), {3}: (12, {})} | custom-call | flops 300000000 | bytes 1000 | tf_op jit(solution)/shard_map/pallas_call | solution.py:102
  270.4 5.2 %shard_map.148 = (bf16[4,128,1024]{2,1,0:T(8,128)(2,1)S(1)}, bf16[4,128,1024]{2,1,0:T(8,128)(2,1)S(1)}, bf16[4,128,1024]{2,1,0:T(8,128)(2,1)S(1)}, bf16[4,128,1024]{2,1,0:T(8,128)(2,1)S(1)}) custom-call(s32[3]{0:T(128)S(1)} %pad_add_fusion.place_ref, bf16[512,688]{1,0:T(8,128)(2,1)S(1)} %copy.70.refs_0_, bf16[512,688]{1,0:T(8,128)(2,1)S(1)} %bitcast.89, ...), custom_call_target="tpu_custom_call" | custom-call | flops 300000000 | bytes 1000 | tf_op jit(solution)/shard_map/pallas_call | solution.py:102
  276.7 10.1 %collective-permute-done.47.refs_5_ = bf16[344,1024]{1,0:T(8,128)(2,1)S(1)} collective-permute-done((bf16[344,1024]{1,0:T(8,128)(2,1)S(1)}, bf16[344,1024]{1,0:T(8,128)(2,1)S(1)}, u32[]{:S(2)}, u32[]{:S(2)}) %collective-permute-start.47) | collective-permute-done | bytes 704544 | tf_op jit(solution)/shard_map/ppermute | solution.py:321
  286.8 5.0 %shard_map.149 = (bf16[4,128,1024]{2,1,0:T(8,128)(2,1)S(1)}, bf16[4,128,1024]{2,1,0:T(8,128)(2,1)S(1)}, bf16[4,128,1024]{2,1,0:T(8,128)(2,1)S(1)}, bf16[4,128,1024]{2,1,0:T(8,128)(2,1)S(1)}) custom-call(s32[3]{0:T(128)S(1)} %pad_add_fusion.place_ref, bf16[512,688]{1,0:T(8,128)(2,1)S(1)} %copy.70.refs_0_, bf16[512,688]{1,0:T(8,128)(2,1)S(1)} %bitcast.90, ...), custom_call_target="tpu_custom_call" | custom-call | flops 300000000 | bytes 1000 | tf_op jit(solution)/shard_map/pallas_call | solution.py:102
  293.4 2.2 collective-permute-done.38
  296.6 1.8 collective-permute-start.50
  298.8 8.9 %collective-permute-done.34 = bf16[2,128,1024]{2,1,0:T(8,128)(2,1)S(1)} collective-permute-done((bf16[2,128,1024]{2,1,0:T(8,128)(2,1)S(1)}, bf16[2,128,1024]{2,1,0:T(8,128)(2,1)S(1)}, u32[]{:S(2)}, u32[]{:S(2)}) %collective-permute-start.34) | collective-permute-done | bytes 524320 | tf_op jit(solution)/shard_map/ppermute | solution.py:321
  308.8 10.6 %collective-permute-done.44 = bf16[4,128,1024]{2,1,0:T(8,128)(2,1)S(1)} collective-permute-done((bf16[4,128,1024]{2,1,0:T(8,128)(2,1)S(1)}, bf16[4,128,1024]{2,1,0:T(8,128)(2,1)S(1)}, u32[]{:S(2)}, u32[]{:S(2)}) %collective-permute-start.44) | collective-permute-done | bytes 1048608 | tf_op jit(solution)/shard_map/ppermute | solution.py:324
  319.8 2.1 collective-permute-start.45
  322.3 18.7 %collective-permute-done.50 = bf16[4,128,1024]{2,1,0:T(8,128)(2,1)S(1)} collective-permute-done((bf16[4,128,1024]{2,1,0:T(8,128)(2,1)S(1)}, bf16[4,128,1024]{2,1,0:T(8,128)(2,1)S(1)}, u32[]{:S(2)}, u32[]{:S(2)}) %collective-permute-start.50) | collective-permute-done | bytes 1048608 | tf_op jit(solution)/shard_map/ppermute | solution.py:324
  341.4 1.8 collective-permute-start.51
  346.6 19.0 %collective-permute-done.51 = bf16[2,128,1024]{2,1,0:T(8,128)(2,1)S(1)} collective-permute-done((bf16[2,128,1024]{2,1,0:T(8,128)(2,1)S(1)}, bf16[2,128,1024]{2,1,0:T(8,128)(2,1)S(1)}, u32[]{:S(2)}, u32[]{:S(2)}) %collective-permute-start.51) | collective-permute-done | bytes 524320 | tf_op jit(solution)/shard_map/ppermute | solution.py:321
  365.8 8.0 %collective-permute-done.46 = bf16[128,1024]{1,0:T(8,128)(2,1)S(1)} collective-permute-done((bf16[128,1024]{1,0:T(8,128)(2,1)S(1)}, bf16[128,1024]{1,0:T(8,128)(2,1)S(1)}, u32[]{:S(2)}, u32[]{:S(2)}) %collective-permute-start.46) | collective-permute-done | bytes 262176 | tf_op jit(solution)/shard_map/ppermute | solution.py:321
  373.9 5.3 %collective-permute-done.52 = bf16[128,1024]{1,0:T(8,128)(2,1)S(1)} collective-permute-done((bf16[128,1024]{1,0:T(8,128)(2,1)S(1)}, bf16[128,1024]{1,0:T(8,128)(2,1)S(1)}, u32[]{:S(2)}, u32[]{:S(2)}) %collective-permute-start.52) | collective-permute-done | bytes 262176 | tf_op jit(solution)/shard_map/ppermute | solution.py:321
  (172 shorter events, 45.3 us)
Async XLA Ops:
  11.8 10.3 %collective-permute-start.14 = (bf16[512,256]{1,0:T(8,128)(2,1)S(1)}, bf16[512,256]{1,0:T(8,128)(2,1)}, u32[]{:S(2)}, u32[]{:S(2)}) collective-permute-start(bf16[512,256]{1,0:T(8,128)(2,1)S(1)} %get-tuple-element.58), channel_id=1, source_target_pairs={{0,8},{4,12},{8,0},{12,4},{16,24},{20,28},{24,16},{28,20},{1,9},{5... | collective-permute-start | bytes 786440 | tf_op jit(solution)/shard_map/ppermute | solution.py:321
  17.7 19.3 %collective-permute-start = (bf16[688,512]{1,0:T(8,128)(2,1)}, bf16[688,512]{1,0:T(8,128)(2,1)S(1)}, u32[]{:S(2)}, u32[]{:S(2)}) collective-permute-start(bf16[688,512]{1,0:T(8,128)(2,1)} %dynamic-slice_bitcast_fusion.4), channel_id=1, source_target_pairs={{0,8},{4,12},{8,0},{12,4},{16,24},{20,28},{24,16},{28,20},{1,9},{5... | collective-permute-start | bytes 2113544 | tf_op jit(solution)/shard_map/ppermute | solution.py:321
  18.6 33.5 %collective-permute-start.1 = (bf16[688,512]{1,0:T(8,128)(2,1)}, bf16[688,512]{1,0:T(8,128)(2,1)S(1)}, u32[]{:S(2)}, u32[]{:S(2)}) collective-permute-start(bf16[688,512]{1,0:T(8,128)(2,1)} %dynamic-slice_bitcast_fusion.3), channel_id=1, source_target_pairs={{0,8},{4,12},{8,0},{12,4},{16,24},{20,28},{24,16},{28,20},{1,9},{5... | collective-permute-start | bytes 2113544 | tf_op jit(solution)/shard_map/ppermute | solution.py:321
  20.6 39.0 %collective-permute-start.10 = (bf16[512,256]{1,0:T(8,128)(2,1)}, bf16[512,256]{1,0:T(8,128)(2,1)}, u32[]{:S(2)}, u32[]{:S(2)}) collective-permute-start(bf16[512,256]{1,0:T(8,128)(2,1)} %get-tuple-element.57), channel_id=1, source_target_pairs={{0,8},{4,12},{8,0},{12,4},{16,24},{20,28},{24,16},{28,20},{1,9},{5... | collective-permute-start | bytes 786440 | tf_op jit(solution)/shard_map/ppermute | solution.py:321
  22.0 7.0 %collective-permute-start.16 = (bf16[512,256]{1,0:T(8,128)(2,1)}, bf16[512,256]{1,0:T(8,128)(2,1)}, u32[]{:S(2)}, u32[]{:S(2)}) collective-permute-start(bf16[512,256]{1,0:T(8,128)(2,1)} %collective-permute-done.14.refs_4_), channel_id=1, source_target_pairs={{0,2},{1,3},{2,0},{3,1},{4,6},{5,7},{6,4},{7,5},{8,10},{9,11},{10,... | collective-permute-start | bytes 786440 | tf_op jit(solution)/shard_map/ppermute | solution.py:324
  24.7 7.3 %collective-permute-start.15 = (bf16[512,256]{1,0:T(8,128)(2,1)}, bf16[512,256]{1,0:T(8,128)(2,1)S(1)}, u32[]{:S(2)}, u32[]{:S(2)}) collective-permute-start(bf16[512,256]{1,0:T(8,128)(2,1)} %collective-permute-done.14.refs_4_), channel_id=1, source_target_pairs={{0,1},{1,0},{2,3},{3,2},{4,5},{5,4},{6,7},{7,6},{8,9},{9,8},{10,11... | collective-permute-start | bytes 786440 | tf_op jit(solution)/shard_map/ppermute | solution.py:324
  29.0 23.1 %collective-permute-start.17 = (bf16[512,256]{1,0:T(8,128)(2,1)}, bf16[512,256]{1,0:T(8,128)(2,1)S(1)}, u32[]{:S(2)}, u32[]{:S(2)}) collective-permute-start(bf16[512,256]{1,0:T(8,128)(2,1)} %collective-permute-done.16.refs_6_), channel_id=1, source_target_pairs={{0,1},{1,0},{2,3},{3,2},{4,5},{5,4},{6,7},{7,6},{8,9},{9,8},{10,11... | collective-permute-start | bytes 786440 | tf_op jit(solution)/shard_map/ppermute | solution.py:324
  32.1 50.1 %collective-permute-start.18 = (bf16[688,512]{1,0:T(8,128)(2,1)S(1)}, bf16[688,512]{1,0:T(8,128)(2,1)S(1)}, u32[]{:S(2)}, u32[]{:S(2)}) collective-permute-start(bf16[688,512]{1,0:T(8,128)(2,1)S(1)} %get-tuple-element.104), channel_id=1, source_target_pairs={{0,24},{4,28},{8,16},{12,20},{16,8},{20,12},{24,0},{28,4},{1,25},{... | collective-permute-start | bytes 2113544 | tf_op jit(solution)/shard_map/ppermute | solution.py:321
  57.5 64.3 %collective-permute-start.20 = (bf16[2,344,1024]{2,1,0:T(8,128)(2,1)S(1)}, bf16[2,344,1024]{2,1,0:T(8,128)(2,1)S(1)}, u32[]{:S(2)}, u32[]{:S(2)}) collective-permute-start(bf16[2,344,1024]{2,1,0:T(8,128)(2,1)S(1)} %get-tuple-element.62), channel_id=1, source_target_pairs={{0,4},{4,0},{8,12},{12,8},{16,20},{20,16},{24,28},{28,24},{1,5},{5... | collective-permute-start | bytes 4227080 | tf_op jit(solution)/shard_map/ppermute | solution.py:321
  59.6 6.6 %collective-permute-start.12 = (bf16[512,256]{1,0:T(8,128)(2,1)}, bf16[512,256]{1,0:T(8,128)(2,1)S(1)}, u32[]{:S(2)}, u32[]{:S(2)}) collective-permute-start(bf16[512,256]{1,0:T(8,128)(2,1)} %collective-permute-done.10.refs_4_), channel_id=1, source_target_pairs={{0,2},{1,3},{2,0},{3,1},{4,6},{5,7},{6,4},{7,5},{8,10},{9,11},{10,... | collective-permute-start | bytes 786440 | tf_op jit(solution)/shard_map/ppermute | solution.py:324
  61.1 6.7 %collective-permute-start.11 = (bf16[512,256]{1,0:T(8,128)(2,1)}, bf16[512,256]{1,0:T(8,128)(2,1)S(1)}, u32[]{:S(2)}, u32[]{:S(2)}) collective-permute-start(bf16[512,256]{1,0:T(8,128)(2,1)} %collective-permute-done.10.refs_4_), channel_id=1, source_target_pairs={{0,1},{1,0},{2,3},{3,2},{4,5},{5,4},{6,7},{7,6},{8,9},{9,8},{10,11... | collective-permute-start | bytes 786440 | tf_op jit(solution)/shard_map/ppermute | solution.py:324
  66.2 15.9 %collective-permute-start.13 = (bf16[512,256]{1,0:T(8,128)(2,1)S(1)}, bf16[512,256]{1,0:T(8,128)(2,1)S(1)}, u32[]{:S(2)}, u32[]{:S(2)}) collective-permute-start(bf16[512,256]{1,0:T(8,128)(2,1)S(1)} %collective-permute-done.12.refs_6_), channel_id=1, source_target_pairs={{0,1},{1,0},{2,3},{3,2},{4,5},{5,4},{6,7},{7,6},{8,9},{9,8},{10,11... | collective-permute-start | bytes 786440 | tf_op jit(solution)/shard_map/ppermute | solution.py:324
  66.2 23.6 %collective-permute-start.6 = (bf16[512,256]{1,0:T(8,128)(2,1)S(1)}, bf16[512,256]{1,0:T(8,128)(2,1)S(1)}, u32[]{:S(2)}, u32[]{:S(2)}) collective-permute-start(bf16[512,256]{1,0:T(8,128)(2,1)S(1)} %copy-done.25), channel_id=1, source_target_pairs={{0,8},{4,12},{8,0},{12,4},{16,24},{20,28},{24,16},{28,20},{1,9},{5... | collective-permute-start | bytes 786440 | tf_op jit(solution)/shard_map/ppermute | solution.py:321
  67.8 45.7 %collective-permute-start.19 = (bf16[688,512]{1,0:T(8,128)(2,1)S(1)}, bf16[688,512]{1,0:T(8,128)(2,1)S(1)}, u32[]{:S(2)}, u32[]{:S(2)}) collective-permute-start(bf16[688,512]{1,0:T(8,128)(2,1)S(1)} %get-tuple-element.106), channel_id=1, source_target_pairs={{0,16},{4,20},{8,24},{12,28},{16,0},{20,4},{24,8},{28,12},{1,17},{... | collective-permute-start | bytes 2113544 | tf_op jit(solution)/shard_map/ppermute | solution.py:321
  88.3 52.3 %collective-permute-start.25 = (bf16[2,344,1024]{2,1,0:T(8,128)(2,1)}, bf16[2,344,1024]{2,1,0:T(8,128)(2,1)}, u32[]{:S(2)}, u32[]{:S(2)}) collective-permute-start(bf16[2,344,1024]{2,1,0:T(8,128)(2,1)} %get-tuple-element.66), channel_id=1, source_target_pairs={{0,4},{4,0},{8,12},{12,8},{16,20},{20,16},{24,28},{28,24},{1,5},{5... | collective-permute-start | bytes 4227080 | tf_op jit(solution)/shard_map/ppermute | solution.py:321
  89.8 7.9 %collective-permute-start.8 = (bf16[512,256]{1,0:T(8,128)(2,1)S(1)}, bf16[512,256]{1,0:T(8,128)(2,1)S(1)}, u32[]{:S(2)}, u32[]{:S(2)}) collective-permute-start(bf16[512,256]{1,0:T(8,128)(2,1)S(1)} %collective-permute-done.6.refs_4_), channel_id=1, source_target_pairs={{0,2},{1,3},{2,0},{3,1},{4,6},{5,7},{6,4},{7,5},{8,10},{9,11},{10,... | collective-permute-start | bytes 786440 | tf_op jit(solution)/shard_map/ppermute | solution.py:324
  97.7 15.8 %collective-permute-start.9 = (bf16[512,256]{1,0:T(8,128)(2,1)S(1)}, bf16[512,256]{1,0:T(8,128)(2,1)S(1)}, u32[]{:S(2)}, u32[]{:S(2)}) collective-permute-start(bf16[512,256]{1,0:T(8,128)(2,1)S(1)} %collective-permute-done.8.refs_6_), channel_id=1, source_target_pairs={{0,1},{1,0},{2,3},{3,2},{4,5},{5,4},{6,7},{7,6},{8,9},{9,8},{10,11... | collective-permute-start | bytes 786440 | tf_op jit(solution)/shard_map/ppermute | solution.py:324
  97.7 22.6 %collective-permute-start.2 = (bf16[512,256]{1,0:T(8,128)(2,1)S(1)}, bf16[512,256]{1,0:T(8,128)(2,1)}, u32[]{:S(2)}, u32[]{:S(2)}) collective-permute-start(bf16[512,256]{1,0:T(8,128)(2,1)S(1)} %copy-done.23), channel_id=1, source_target_pairs={{0,8},{4,12},{8,0},{12,4},{16,24},{20,28},{24,16},{28,20},{1,9},{5... | collective-permute-start | bytes 786440 | tf_op jit(solution)/shard_map/ppermute | solution.py:321
  118.7 62.2 %collective-permute-start.23 = (bf16[2,344,1024]{2,1,0:T(8,128)(2,1)}, bf16[2,344,1024]{2,1,0:T(8,128)(2,1)}, u32[]{:S(2)}, u32[]{:S(2)}) collective-permute-start(bf16[2,344,1024]{2,1,0:T(8,128)(2,1)} %get-tuple-element.65), channel_id=1, source_target_pairs={{0,4},{4,0},{8,12},{12,8},{16,20},{20,16},{24,28},{28,24},{1,5},{5... | collective-permute-start | bytes 4227080 | tf_op jit(solution)/shard_map/ppermute | solution.py:321
  120.3 7.9 %collective-permute-start.4 = (bf16[512,256]{1,0:T(8,128)(2,1)}, bf16[512,256]{1,0:T(8,128)(2,1)}, u32[]{:S(2)}, u32[]{:S(2)}) collective-permute-start(bf16[512,256]{1,0:T(8,128)(2,1)} %collective-permute-done.2.refs_4_), channel_id=1, source_target_pairs={{0,2},{1,3},{2,0},{3,1},{4,6},{5,7},{6,4},{7,5},{8,10},{9,11},{10,... | collective-permute-start | bytes 786440 | tf_op jit(solution)/shard_map/ppermute | solution.py:324
  123.5 34.7 %collective-permute-start.27 = (bf16[344,1024]{1,0:T(8,128)(2,1)}, bf16[344,1024]{1,0:T(8,128)(2,1)}, u32[]{:S(2)}, u32[]{:S(2)}) collective-permute-start(bf16[344,1024]{1,0:T(8,128)(2,1)} %get-tuple-element.108.refs_10_), channel_id=1, source_target_pairs={{0,16},{4,20},{8,24},{12,28},{16,0},{20,4},{24,8},{28,12},{1,17},{... | collective-permute-start | bytes 2113544 | tf_op jit(solution)/shard_map/ppermute | solution.py:321
  128.2 51.3 %collective-permute-start.28 = (bf16[688,512]{1,0:T(8,128)(2,1)}, bf16[688,512]{1,0:T(8,128)(2,1)}, u32[]{:S(2)}, u32[]{:S(2)}) collective-permute-start(bf16[688,512]{1,0:T(8,128)(2,1)} %get-tuple-element.103), channel_id=1, source_target_pairs={{0,8},{4,12},{8,0},{12,4},{16,24},{20,28},{24,16},{28,20},{1,9},{5... | collective-permute-start | bytes 2113544 | tf_op jit(solution)/shard_map/ppermute | solution.py:321
  140.0 74.7 %collective-permute-start.21 = (bf16[2,344,1024]{2,1,0:T(8,128)(2,1)}, bf16[2,344,1024]{2,1,0:T(8,128)(2,1)}, u32[]{:S(2)}, u32[]{:S(2)}) collective-permute-start(bf16[2,344,1024]{2,1,0:T(8,128)(2,1)} %get-tuple-element.64), channel_id=1, source_target_pairs={{0,4},{4,0},{8,12},{12,8},{16,20},{20,16},{24,28},{28,24},{1,5},{5... | collective-permute-start | bytes 4227080 | tf_op jit(solution)/shard_map/ppermute | solution.py:321
  143.6 58.3 %collective-permute-start.26 = (bf16[344,1024]{1,0:T(8,128)(2,1)}, bf16[344,1024]{1,0:T(8,128)(2,1)}, u32[]{:S(2)}, u32[]{:S(2)}) collective-permute-start(bf16[344,1024]{1,0:T(8,128)(2,1)} %get-tuple-element.109.refs_9_), channel_id=1, source_target_pairs={{0,16},{4,20},{8,24},{12,28},{16,0},{20,4},{24,8},{28,12},{1,17},{... | collective-permute-start | bytes 2113544 | tf_op jit(solution)/shard_map/ppermute | solution.py:321
  164.1 44.5 %collective-permute-start.29 = (bf16[344,1024]{1,0:T(8,128)(2,1)}, bf16[344,1024]{1,0:T(8,128)(2,1)}, u32[]{:S(2)}, u32[]{:S(2)}) collective-permute-start(bf16[344,1024]{1,0:T(8,128)(2,1)} %get-tuple-element.71.refs_12_.refs_4_), channel_id=1, source_target_pairs={{0,4},{4,0},{8,12},{12,8},{16,20},{20,16},{24,28},{28,24},{1,5},{5... | collective-permute-start | bytes 2113544 | tf_op jit(solution)/shard_map/ppermute | solution.py:321
  183.3 33.4 %collective-permute-start.24 = (bf16[344,1024]{1,0:T(8,128)(2,1)S(1)}, bf16[344,1024]{1,0:T(8,128)(2,1)S(1)}, u32[]{:S(2)}, u32[]{:S(2)}) collective-permute-start(bf16[344,1024]{1,0:T(8,128)(2,1)S(1)} %get-tuple-element.111.refs_14_), channel_id=1, source_target_pairs={{0,16},{4,20},{8,24},{12,28},{16,0},{20,4},{24,8},{28,12},{1,17},{... | collective-permute-start | bytes 2113544 | tf_op jit(solution)/shard_map/ppermute | solution.py:321
  207.5 17.6 %collective-permute-start.30 = (bf16[344,1024]{1,0:T(8,128)(2,1)S(1)}, bf16[344,1024]{1,0:T(8,128)(2,1)S(1)}, u32[]{:S(2)}, u32[]{:S(2)}) collective-permute-start(bf16[344,1024]{1,0:T(8,128)(2,1)S(1)} %get-tuple-element.76.refs_6_.refs_4_), channel_id=1, source_target_pairs={{0,4},{4,0},{8,12},{12,8},{16,20},{20,16},{24,28},{28,24},{1,5},{5... | collective-permute-start | bytes 2113544 | tf_op jit(solution)/shard_map/ppermute | solution.py:321
  214.6 16.1 %collective-permute-start.31 = (bf16[4,128,1024]{2,1,0:T(8,128)(2,1)S(1)}, bf16[4,128,1024]{2,1,0:T(8,128)(2,1)S(1)}, u32[]{:S(2)}, u32[]{:S(2)}) collective-permute-start(bf16[4,128,1024]{2,1,0:T(8,128)(2,1)S(1)} %get-tuple-element.85), channel_id=1, source_target_pairs={{0,1},{1,0},{2,3},{3,2},{4,5},{5,4},{6,7},{7,6},{8,9},{9,8},{10,11... | collective-permute-start | bytes 3145736 | tf_op jit(solution)/shard_map/ppermute | solution.py:324
  230.1 38.6 %collective-permute-start.37 = (bf16[4,128,1024]{2,1,0:T(8,128)(2,1)S(1)}, bf16[4,128,1024]{2,1,0:T(8,128)(2,1)S(1)}, u32[]{:S(2)}, u32[]{:S(2)}) collective-permute-start(bf16[4,128,1024]{2,1,0:T(8,128)(2,1)S(1)} %get-tuple-element.93), channel_id=1, source_target_pairs={{0,1},{1,0},{2,3},{3,2},{4,5},{5,4},{6,7},{7,6},{8,9},{9,8},{10,11... | collective-permute-start | bytes 3145736 | tf_op jit(solution)/shard_map/ppermute | solution.py:324
  230.2 32.9 %collective-permute-start.22 = (bf16[344,1024]{1,0:T(8,128)(2,1)S(1)}, bf16[344,1024]{1,0:T(8,128)(2,1)S(1)}, u32[]{:S(2)}, u32[]{:S(2)}) collective-permute-start(bf16[344,1024]{1,0:T(8,128)(2,1)S(1)} %get-tuple-element.113.refs_13_), channel_id=1, source_target_pairs={{0,16},{4,20},{8,24},{12,28},{16,0},{20,4},{24,8},{28,12},{1,17},{... | collective-permute-start | bytes 2113544 | tf_op jit(solution)/shard_map/ppermute | solution.py:321
  230.2 45.4 %collective-permute-start.32 = (bf16[4,128,1024]{2,1,0:T(8,128)(2,1)S(1)}, bf16[4,128,1024]{2,1,0:T(8,128)(2,1)S(1)}, u32[]{:S(2)}, u32[]{:S(2)}) collective-permute-start(bf16[4,128,1024]{2,1,0:T(8,128)(2,1)S(1)} %get-tuple-element.90), channel_id=1, source_target_pairs={{0,1},{1,0},{2,3},{3,2},{4,5},{5,4},{6,7},{7,6},{8,9},{9,8},{10,11... | collective-permute-start | bytes 3145736 | tf_op jit(solution)/shard_map/ppermute | solution.py:324
  231.1 45.2 %collective-permute-start.33 = (bf16[4,128,1024]{2,1,0:T(8,128)(2,1)S(1)}, bf16[4,128,1024]{2,1,0:T(8,128)(2,1)S(1)}, u32[]{:S(2)}, u32[]{:S(2)}) collective-permute-start(bf16[4,128,1024]{2,1,0:T(8,128)(2,1)S(1)} %add_convert_fusion.7.refs_13_), channel_id=1, source_target_pairs={{0,2},{1,3},{2,0},{3,1},{4,6},{5,7},{6,4},{7,5},{8,10},{9,11},{10,... | collective-permute-start | bytes 3145736 | tf_op jit(solution)/shard_map/ppermute | solution.py:324
  231.6 38.7 %collective-permute-start.41 = (bf16[344,1024]{1,0:T(8,128)(2,1)S(1)}, bf16[344,1024]{1,0:T(8,128)(2,1)S(1)}, u32[]{:S(2)}, u32[]{:S(2)}) collective-permute-start(bf16[344,1024]{1,0:T(8,128)(2,1)S(1)} %get-tuple-element.82.refs_6_.refs_4_), channel_id=1, source_target_pairs={{0,4},{4,0},{8,12},{12,8},{16,20},{20,16},{24,28},{28,24},{1,5},{5... | collective-permute-start | bytes 2113544 | tf_op jit(solution)/shard_map/ppermute | solution.py:321
  263.1 29.4 %collective-permute-start.36 = (bf16[4,128,1024]{2,1,0:T(8,128)(2,1)S(1)}, bf16[4,128,1024]{2,1,0:T(8,128)(2,1)S(1)}, u32[]{:S(2)}, u32[]{:S(2)}) collective-permute-start(bf16[4,128,1024]{2,1,0:T(8,128)(2,1)S(1)} %get-tuple-element.91), channel_id=1, source_target_pairs={{0,1},{1,0},{2,3},{3,2},{4,5},{5,4},{6,7},{7,6},{8,9},{9,8},{10,11... | collective-permute-start | bytes 3145736 | tf_op jit(solution)/shard_map/ppermute | solution.py:324
  268.6 18.2 %collective-permute-start.47 = (bf16[344,1024]{1,0:T(8,128)(2,1)S(1)}, bf16[344,1024]{1,0:T(8,128)(2,1)S(1)}, u32[]{:S(2)}, u32[]{:S(2)}) collective-permute-start(bf16[344,1024]{1,0:T(8,128)(2,1)S(1)} %get-tuple-element.94.refs_6_.refs_4_), channel_id=1, source_target_pairs={{0,4},{4,0},{8,12},{12,8},{16,20},{20,16},{24,28},{28,24},{1,5},{5... | collective-permute-start | bytes 2113544 | tf_op jit(solution)/shard_map/ppermute | solution.py:321
  270.3 25.3 %collective-permute-start.38 = (bf16[4,128,1024]{2,1,0:T(8,128)(2,1)S(1)}, bf16[4,128,1024]{2,1,0:T(8,128)(2,1)S(1)}, u32[]{:S(2)}, u32[]{:S(2)}) collective-permute-start(bf16[4,128,1024]{2,1,0:T(8,128)(2,1)S(1)} %add_convert_fusion.4.refs_7_), channel_id=1, source_target_pairs={{0,2},{1,3},{2,0},{3,1},{4,6},{5,7},{6,4},{7,5},{8,10},{9,11},{10,... | collective-permute-start | bytes 3145736 | tf_op jit(solution)/shard_map/ppermute | solution.py:324
  275.6 17.3 %collective-permute-start.43 = (bf16[4,128,1024]{2,1,0:T(8,128)(2,1)S(1)}, bf16[4,128,1024]{2,1,0:T(8,128)(2,1)S(1)}, u32[]{:S(2)}, u32[]{:S(2)}) collective-permute-start(bf16[4,128,1024]{2,1,0:T(8,128)(2,1)S(1)} %get-tuple-element.98), channel_id=1, source_target_pairs={{0,1},{1,0},{2,3},{3,2},{4,5},{5,4},{6,7},{7,6},{8,9},{9,8},{10,11... | collective-permute-start | bytes 3145736 | tf_op jit(solution)/shard_map/ppermute | solution.py:324
  292.8 14.8 %collective-permute-start.34 = (bf16[2,128,1024]{2,1,0:T(8,128)(2,1)S(1)}, bf16[2,128,1024]{2,1,0:T(8,128)(2,1)S(1)}, u32[]{:S(2)}, u32[]{:S(2)}) collective-permute-start(bf16[2,128,1024]{2,1,0:T(8,128)(2,1)S(1)} %get-tuple-element.118.refs_8_), channel_id=1, source_target_pairs={{0,8},{4,12},{8,0},{12,4},{16,24},{20,28},{24,16},{28,20},{1,9},{5... | collective-permute-start | bytes 1572872 | tf_op jit(solution)/shard_map/ppermute | solution.py:321
  293.3 26.1 %collective-permute-start.44 = (bf16[4,128,1024]{2,1,0:T(8,128)(2,1)S(1)}, bf16[4,128,1024]{2,1,0:T(8,128)(2,1)S(1)}, u32[]{:S(2)}, u32[]{:S(2)}) collective-permute-start(bf16[4,128,1024]{2,1,0:T(8,128)(2,1)S(1)} %add_convert_fusion.2), channel_id=1, source_target_pairs={{0,2},{1,3},{2,0},{3,1},{4,6},{5,7},{6,4},{7,5},{8,10},{9,11},{10,... | collective-permute-start | bytes 3145736 | tf_op jit(solution)/shard_map/ppermute | solution.py:324
  296.0 47.2 %collective-permute-start.39 = (bf16[2,128,1024]{2,1,0:T(8,128)(2,1)S(1)}, bf16[2,128,1024]{2,1,0:T(8,128)(2,1)S(1)}, u32[]{:S(2)}, u32[]{:S(2)}) collective-permute-start(bf16[2,128,1024]{2,1,0:T(8,128)(2,1)S(1)} %get-tuple-element.120), channel_id=1, source_target_pairs={{0,8},{4,12},{8,0},{12,4},{16,24},{20,28},{24,16},{28,20},{1,9},{5... | collective-permute-start | bytes 1572872 | tf_op jit(solution)/shard_map/ppermute | solution.py:321
  296.1 25.8 %collective-permute-start.48 = (bf16[4,128,1024]{2,1,0:T(8,128)(2,1)S(1)}, bf16[4,128,1024]{2,1,0:T(8,128)(2,1)S(1)}, u32[]{:S(2)}, u32[]{:S(2)}) collective-permute-start(bf16[4,128,1024]{2,1,0:T(8,128)(2,1)S(1)} %get-tuple-element.100), channel_id=1, source_target_pairs={{0,1},{1,0},{2,3},{3,2},{4,5},{5,4},{6,7},{7,6},{8,9},{9,8},{10,11... | collective-permute-start | bytes 3145736 | tf_op jit(solution)/shard_map/ppermute | solution.py:324
  296.6 44.4 %collective-permute-start.50 = (bf16[4,128,1024]{2,1,0:T(8,128)(2,1)S(1)}, bf16[4,128,1024]{2,1,0:T(8,128)(2,1)S(1)}, u32[]{:S(2)}, u32[]{:S(2)}) collective-permute-start(bf16[4,128,1024]{2,1,0:T(8,128)(2,1)S(1)} %add_convert_fusion), channel_id=1, source_target_pairs={{0,2},{1,3},{2,0},{3,1},{4,6},{5,7},{6,4},{7,5},{8,10},{9,11},{10,... | collective-permute-start | bytes 3145736 | tf_op jit(solution)/shard_map/ppermute | solution.py:324
  307.7 36.9 %collective-permute-start.35 = (bf16[128,1024]{1,0:T(8,128)(2,1)S(1)}, bf16[128,1024]{1,0:T(8,128)(2,1)S(1)}, u32[]{:S(2)}, u32[]{:S(2)}) collective-permute-start(bf16[128,1024]{1,0:T(8,128)(2,1)S(1)} %fusion.13), channel_id=1, source_target_pairs={{0,16},{4,20},{8,24},{12,28},{16,0},{20,4},{24,8},{28,12},{1,17},{... | collective-permute-start | bytes 786440 | tf_op jit(solution)/shard_map/ppermute | solution.py:321
  319.8 25.0 %collective-permute-start.45 = (bf16[2,128,1024]{2,1,0:T(8,128)(2,1)S(1)}, bf16[2,128,1024]{2,1,0:T(8,128)(2,1)S(1)}, u32[]{:S(2)}, u32[]{:S(2)}) collective-permute-start(bf16[2,128,1024]{2,1,0:T(8,128)(2,1)S(1)} %get-tuple-element.122), channel_id=1, source_target_pairs={{0,8},{4,12},{8,0},{12,4},{16,24},{20,28},{24,16},{28,20},{1,9},{5... | collective-permute-start | bytes 1572872 | tf_op jit(solution)/shard_map/ppermute | solution.py:321
  341.4 24.1 %collective-permute-start.51 = (bf16[2,128,1024]{2,1,0:T(8,128)(2,1)S(1)}, bf16[2,128,1024]{2,1,0:T(8,128)(2,1)S(1)}, u32[]{:S(2)}, u32[]{:S(2)}) collective-permute-start(bf16[2,128,1024]{2,1,0:T(8,128)(2,1)S(1)} %get-tuple-element.124), channel_id=1, source_target_pairs={{0,8},{4,12},{8,0},{12,4},{16,24},{20,28},{24,16},{28,20},{1,9},{5... | collective-permute-start | bytes 1572872 | tf_op jit(solution)/shard_map/ppermute | solution.py:321
  343.3 22.4 %collective-permute-start.40 = (bf16[128,1024]{1,0:T(8,128)(2,1)S(1)}, bf16[128,1024]{1,0:T(8,128)(2,1)S(1)}, u32[]{:S(2)}, u32[]{:S(2)}) collective-permute-start(bf16[128,1024]{1,0:T(8,128)(2,1)S(1)} %fusion.15), channel_id=1, source_target_pairs={{0,16},{4,20},{8,24},{12,28},{16,0},{20,4},{24,8},{28,12},{1,17},{... | collective-permute-start | bytes 786440 | tf_op jit(solution)/shard_map/ppermute | solution.py:321
  344.9 28.9 %collective-permute-start.46 = (bf16[128,1024]{1,0:T(8,128)(2,1)S(1)}, bf16[128,1024]{1,0:T(8,128)(2,1)S(1)}, u32[]{:S(2)}, u32[]{:S(2)}) collective-permute-start(bf16[128,1024]{1,0:T(8,128)(2,1)S(1)} %fusion.17), channel_id=1, source_target_pairs={{0,16},{4,20},{8,24},{12,28},{16,0},{20,4},{24,8},{28,12},{1,17},{... | collective-permute-start | bytes 786440 | tf_op jit(solution)/shard_map/ppermute | solution.py:321
  365.6 13.6 %collective-permute-start.52 = (bf16[128,1024]{1,0:T(8,128)(2,1)S(1)}, bf16[128,1024]{1,0:T(8,128)(2,1)S(1)}, u32[]{:S(2)}, u32[]{:S(2)}) collective-permute-start(bf16[128,1024]{1,0:T(8,128)(2,1)S(1)} %fusion.19), channel_id=1, source_target_pairs={{0,16},{4,20},{8,24},{12,28},{16,0},{20,4},{24,8},{28,12},{1,17},{... | collective-permute-start | bytes 786440 | tf_op jit(solution)/shard_map/ppermute | solution.py:321
  (34 other events, 368.0 us)
where the time goes:
time: 381 us; the launch traced here: 380 us
  waiting for transfers between devices  203 us (53%)
  Pallas kernels  70.4 us (18%)
  starting transfers between devices  69 us (18%)
  local copies, waits for them, and re-layouts  19.7 us (5%)
  other arithmetic  16.5 us (4%)
    ppermute x29, waiting for transfers between devices, over_dp(): return lax.ppermute(value, 'dp', [(i, i ^ bits) for i in range(dp_size)])  150 us
    pallas_call x13, Pallas kernels, __call__(): pl.pallas_call(wrapped, grid_spec=pltpu.PrefetchScalarGridSpec(num_scalar...  70.4 us
    ppermute x29, starting transfers between devices, over_dp(): return lax.ppermute(value, 'dp', [(i, i ^ bits) for i in range(dp_size)])  58.4 us
    ppermute x24, waiting for transfers between devices, over_tensor(): lax.ppermute(value, 'tensor', [(i, i ^ bits) for i in range(tensor_size)])  53.5 us
    convert_element_type x24, other arithmetic, add(): return (a.astype(jnp.float32) + b.astype(jnp.float32)).astype(jnp.bfloat16)  14.5 us
    ppermute x24, starting transfers between devices, over_tensor(): lax.ppermute(value, 'tensor', [(i, i ^ bits) for i in range(tensor_size)])  10.6 us
    unnamed x59, local copies, waits for them, and re-layouts  10.4 us
  transfers between devices with their start and end apart: 53, of which 22 were waited for; matrix products, arithmetic and copies ran while one was open for 6% of the time, Pallas kernels for 18%

commit v1 on v0

--- a/solution.py
+++ b/solution.py
@@ -37,8 +37,8 @@
     "ay1",
     "ad0",
     "tu1",
+    "ad1",
     "ay2",
-    "ad1",
     "g20",
     "ay3",
     "ad2",
@@ -55,11 +55,11 @@
     "sc3",
     "sx2",
     "sn1",
+    "sn2",
     "sx3",
-    "sn2",
     "sn3",
 )
-COST = {"ro": 300000000, "st": 25000000000, "ay": 300000000, "g1": 300000000, "ad": 300000000, "tu": 300000000, "g2": 300000000, "sc": 300000000, "sx": 300000000, "sn": 300000000}
+COST = {"ro": 300000000, "st": 25000000000, "ay": 300000000, "g1": 300000000, "ad": 300000000, "tu": 300000000, "g2": 300000000, "sc": 300000000, "sx": 300000000, "sn": 300000000, "ad1": 1000000, "g12": 3000000000}
 VMEM_BYTES = 28 * 1024 * 1024
 
 
@@ -111,7 +111,7 @@
             out_shape=out_shape,
             input_output_aliases=aliases or {},
             compiler_params=pltpu.CompilerParams(vmem_limit_bytes=VMEM_BYTES),
-            cost_estimate=pl.CostEstimate(flops=COST[name[:2]], bytes_accessed=1000, transcendentals=0),
+            cost_estimate=pl.CostEstimate(flops=COST.get(name, COST[name[:2]]), bytes_accessed=1000, transcendentals=0),
         )(self.place, *args, *held)
         self.held = [outs[token]]
         return outs

time: 381 us -> 381 us (level)
  starting transfers between devices: 69 us -> 47.2 us
  local copies, waits for them, and re-layouts: 19.7 us -> 31.2 us
  waiting for transfers between devices: 203 us -> 211 us
    ppermute x29, starting transfers between devices: 58.4 us -> 34.2 us  [over_dp(): return lax.ppermute(value, 'dp', [(i, i ^ bits) for i in range(dp_size)])]
    ppermute x29, waiting for transfers between devices: 150 us -> 173 us  [over_dp(): return lax.ppermute(value, 'dp', [(i, i ^ bits) for i in range(dp_size)])]
    ppermute x24, waiting for transfers between devices: 53.5 us -> 37.7 us  [over_tensor(): lax.ppermute(value, 'tensor', [(i, i ^ bits) for i in range(tensor_size)])]
    unnamed x59 -> x65, local copies, waits for them, and re-layouts: 10.4 us -> 14.9 us
  transfers between devices with their start and end apart: 53 -> 53, of which waited for: 22 -> 20; matrix products, arithmetic and copies ran while one was open for 6% -> 8% of each run, Pallas kernels for 18% -> 18%
where the time goes in v1:
time: 381 us; the launch traced here: 380 us
  waiting for transfers between devices  211 us (55%)
  Pallas kernels  71.8 us (19%)
  starting transfers between devices  47.2 us (12%)
  local copies, waits for them, and re-layouts  31.2 us (8%)
  other arithmetic  17.6 us (5%)
    ppermute x29, waiting for transfers between devices, over_dp(): return lax.ppermute(value, 'dp', [(i, i ^ bits) for i in range(dp_size)])  173 us
    pallas_call x13, Pallas kernels, __call__(): pl.pallas_call(wrapped, grid_spec=pltpu.PrefetchScalarGridSpec(num_scalar...  71.8 us
    ppermute x24, waiting for transfers between devices, over_tensor(): lax.ppermute(value, 'tensor', [(i, i ^ bits) for i in range(tensor_size)])  37.7 us
    ppermute x29, starting transfers between devices, over_dp(): return lax.ppermute(value, 'dp', [(i, i ^ bits) for i in range(dp_size)])  34.2 us
    convert_element_type x24, other arithmetic, add(): return (a.astype(jnp.float32) + b.astype(jnp.float32)).astype(jnp.bfloat16)  15.6 us
    unnamed x65, local copies, waits for them, and re-layouts  14.9 us
    ppermute x24, starting transfers between devices, over_tensor(): lax.ppermute(value, 'tensor', [(i, i ^ bits) for i in range(tensor_size)])  13 us
  transfers between devices with their start and end apart: 53, of which 20 were waited for; matrix products, arithmetic and copies ran while one was open for 8% of the time, Pallas kernels for 18%

profile of v1, /device:TPU:0, one launch (start us, length us, event | category | flops | bytes accessed | tf_op | source)
XLA Modules:
  0.0 379.9 jit_solution(13910790907382952395)
XLA Ops:
  1.5 2.2 copy-done.10
  4.6 3.8 shard_map.137
  8.4 2.0 copy-done
  10.4 3.0 collective-permute-start.14
  13.4 3.0 fusion.21
  17.6 2.0 dynamic-slice_bitcast_fusion.3
  19.6 1.8 collective-permute-start.1
  21.8 1.8 collective-permute-start.16
  24.6 3.3 dynamic-slice_bitcast_fusion
  30.0 3.6 collective-permute-start.18
  36.3 15.2 %collective-permute-done.1.refs_2_ = bf16[688,512]{1,0:T(8,128)(2,1)} collective-permute-done((bf16[688,512]{1,0:T(8,128)(2,1)}, bf16[688,512]{1,0:T(8,128)(2,1)}, u32[]{:S(2)}, u32[]{:S(2)}) %collective-permute-start.1) | collective-permute-done | bytes 704544 | tf_op jit(solution)/shard_map/ppermute | solution.py:321
  51.5 2.2 copy-done.1
  55.6 5.5 %shard_map.138 = (bf16[2,344,1024]{2,1,0:T(8,128)(2,1)S(1)}, bf16[2,344,1024]{2,1,0:T(8,128)(2,1)S(1)}) custom-call(s32[3]{0:T(128)S(1)} %pad_add_fusion.place_ref, bf16[1376,512]{1,0:T(8,128)(2,1)S(1)} %bitcast.75, bf16[688,512]{1,0:T(8,128)(2,1)S(1)} %collective-permute-done.refs_1_, bf16[688,512]{1,0:T(8,128)(2,1)} %collective-permute-done.1.refs_2_, ...), custom_call_target="tpu_custom_call" | custom-call | flops 300000000 | bytes 1000 | tf_op jit(solution)/shard_map/pallas_call | solution.py:102
  65.6 3.7 collective-permute-done.12.refs_6_
  69.3 9.2 %collective-permute-done.6.refs_4_ = bf16[512,256]{1,0:T(8,128)(2,1)S(1)} collective-permute-done((bf16[512,256]{1,0:T(8,128)(2,1)S(1)}, bf16[512,256]{1,0:T(8,128)(2,1)S(1)}, u32[]{:S(2)}, u32[]{:S(2)}) %collective-permute-start.6) | collective-permute-done | bytes 262176 | tf_op jit(solution)/shard_map/ppermute | solution.py:321
  80.1 2.0 collective-permute-start.2
  82.7 6.2 %shard_map.139 = (bf16[2,344,1024]{2,1,0:T(8,128)(2,1)S(1)}, bf16[2,344,1024]{2,1,0:T(8,128)(2,1)}) custom-call(s32[3]{0:T(128)S(1)} %pad_add_fusion.place_ref, bf16[1376,512]{1,0:T(8,128)(2,1)S(1)} %bitcast.76, bf16[688,512]{1,0:T(8,128)(2,1)S(1)} %collective-permute-done.refs_1_, bf16[688,512]{1,0:T(8,128)(2,1)} %collective-permute-done.1.refs_2_, ...), custom_call_target="tpu_custom_call" | custom-call | flops 300000000 | bytes 1000 | tf_op jit(solution)/shard_map/pallas_call | solution.py:102
  90.4 9.2 %collective-permute-done.2.refs_4_ = bf16[512,256]{1,0:T(8,128)(2,1)} collective-permute-done((bf16[512,256]{1,0:T(8,128)(2,1)S(1)}, bf16[512,256]{1,0:T(8,128)(2,1)}, u32[]{:S(2)}, u32[]{:S(2)}) %collective-permute-start.2) | collective-permute-done | bytes 262176 | tf_op jit(solution)/shard_map/ppermute | solution.py:321
  102.7 9.2 %collective-permute-done.19.refs_10_ = bf16[688,512]{1,0:T(8,128)(2,1)S(1)} collective-permute-done((bf16[688,512]{1,0:T(8,128)(2,1)S(1)}, bf16[688,512]{1,0:T(8,128)(2,1)S(1)}, u32[]{:S(2)}, u32[]{:S(2)}) %collective-permute-start.19) | collective-permute-done | bytes 704544 | tf_op jit(solution)/shard_map/ppermute | solution.py:321
  111.8 6.2 %shard_map.140 = (bf16[2,344,1024]{2,1,0:T(8,128)(2,1)S(1)}, bf16[2,344,1024]{2,1,0:T(8,128)(2,1)}) custom-call(s32[3]{0:T(128)S(1)} %pad_add_fusion.place_ref, bf16[1376,512]{1,0:T(8,128)(2,1)S(1)} %bitcast.77, bf16[688,512]{1,0:T(8,128)(2,1)S(1)} %collective-permute-done.refs_1_, bf16[688,512]{1,0:T(8,128)(2,1)} %collective-permute-done.1.refs_2_, ...), custom_call_target="tpu_custom_call" | custom-call | flops 3000000000 | bytes 1000 | tf_op jit(solution)/shard_map/pallas_call | solution.py:102
  123.2 1.9 collective-permute-start.28
  125.2 2.2 copy-done.2
  128.7 6.5 %shard_map.141 = (bf16[2,344,1024]{2,1,0:T(8,128)(2,1)S(1)}, bf16[2,344,1024]{2,1,0:T(8,128)(2,1)}) custom-call(s32[3]{0:T(128)S(1)} %pad_add_fusion.place_ref, bf16[1376,512]{1,0:T(8,128)(2,1)S(1)} %bitcast.78, bf16[688,512]{1,0:T(8,128)(2,1)S(1)} %collective-permute-done.refs_1_, bf16[688,512]{1,0:T(8,128)(2,1)} %collective-permute-done.1.refs_2_, ...), custom_call_target="tpu_custom_call" | custom-call | flops 300000000 | bytes 1000 | tf_op jit(solution)/shard_map/pallas_call | solution.py:102
  135.8 3.2 fusion.6
  140.3 14.7 %collective-permute-done.27.refs_1_ = bf16[344,1024]{1,0:T(8,128)(2,1)} collective-permute-done((bf16[344,1024]{1,0:T(8,128)(2,1)}, bf16[344,1024]{1,0:T(8,128)(2,1)}, u32[]{:S(2)}, u32[]{:S(2)}) %collective-permute-start.27) | collective-permute-done | bytes 704544 | tf_op jit(solution)/shard_map/ppermute | solution.py:321
  155.0 5.8 %shard_map.142 = (f32[344,4096]{1,0:T(8,128)}, f32[344,4096]{1,0:T(8,128)}, f32[344,4096]{1,0:T(8,128)}, f32[344,4096]{1,0:T(8,128)}, bf16[344,1024]{1,0:T(8,128)(2,1)}) custom-call(s32[3]{0:T(128)S(1)} %pad_add_fusion.place_ref, bf16[344,1024]{1,0:T(8,128)(2,1)S(1)} %copy-done.14, bf16[344,1024]{1,0:T(8,128)(2,1)} %collective-permute-done.27.refs_1_, ...), custom_call_target="tpu_custom_call" | custom-call | flops 300000000 | bytes 1000 | tf_op jit(solution)/shard_map/pallas_call | solution.py:102
  161.3 3.0 fusion.4
  168.8 30.5 %collective-permute-done.26.refs_1_ = bf16[344,1024]{1,0:T(8,128)(2,1)} collective-permute-done((bf16[344,1024]{1,0:T(8,128)(2,1)}, bf16[344,1024]{1,0:T(8,128)(2,1)}, u32[]{:S(2)}, u32[]{:S(2)}) %collective-permute-start.26) | collective-permute-done | bytes 704544 | tf_op jit(solution)/shard_map/ppermute | solution.py:321
  200.3 5.6 %shard_map.143 = (f32[344,4096]{1,0:T(8,128)}, f32[344,4096]{1,0:T(8,128)}, f32[344,4096]{1,0:T(8,128)}, f32[344,4096]{1,0:T(8,128)}, bf16[344,1024]{1,0:T(8,128)(2,1)S(1)}) custom-call(s32[3]{0:T(128)S(1)} %pad_add_fusion.place_ref, bf16[344,1024]{1,0:T(8,128)(2,1)S(1)} %copy-done.15, ...), custom_call_target="tpu_custom_call", output_to_operand_aliasing={{0}: (9, {}), {1}: (10, {}), {2}: (11, {}), {3}: (12, {})} | custom-call | flops 1000000 | bytes 1000 | tf_op jit(solution)/shard_map/pallas_call | solution.py:102
  206.5 6.0 %shard_map.144 = (bf16[4,128,1024]{2,1,0:T(8,128)(2,1)S(1)}, bf16[4,128,1024]{2,1,0:T(8,128)(2,1)S(1)}, bf16[4,128,1024]{2,1,0:T(8,128)(2,1)S(1)}, bf16[4,128,1024]{2,1,0:T(8,128)(2,1)S(1)}) custom-call(s32[3]{0:T(128)S(1)} %pad_add_fusion.place_ref, bf16[512,688]{1,0:T(8,128)(2,1)S(1)} %copy.70.refs_0_, bf16[512,688]{1,0:T(8,128)(2,1)S(1)} %bitcast.87, ...), custom_call_target="tpu_custom_call" | custom-call | flops 300000000 | bytes 1000 | tf_op jit(solution)/shard_map/pallas_call | solution.py:102
  212.6 2.0 fusion.2
  214.5 5.6 %shard_map.145 = (f32[344,4096]{1,0:T(8,128)}, f32[344,4096]{1,0:T(8,128)}, f32[344,4096]{1,0:T(8,128)}, f32[344,4096]{1,0:T(8,128)}, bf16[344,1024]{1,0:T(8,128)(2,1)S(1)}) custom-call(s32[3]{0:T(128)S(1)} %pad_add_fusion.place_ref, bf16[344,1024]{1,0:T(8,128)(2,1)S(1)} %copy-done.13, ...), custom_call_target="tpu_custom_call", output_to_operand_aliasing={{0}: (9, {}), {1}: (10, {}), {2}: (11, {}), {3}: (12, {})} | custom-call | flops 300000000 | bytes 1000 | tf_op jit(solution)/shard_map/pallas_call | solution.py:102
  220.2 3.4 collective-permute-done.30.refs_5_
  223.6 5.0 %shard_map.146 = (bf16[4,128,1024]{2,1,0:T(8,128)(2,1)S(1)}, bf16[4,128,1024]{2,1,0:T(8,128)(2,1)S(1)}, bf16[4,128,1024]{2,1,0:T(8,128)(2,1)S(1)}, bf16[4,128,1024]{2,1,0:T(8,128)(2,1)S(1)}) custom-call(s32[3]{0:T(128)S(1)} %pad_add_fusion.place_ref, bf16[512,688]{1,0:T(8,128)(2,1)S(1)} %copy.70.refs_0_, bf16[512,688]{1,0:T(8,128)(2,1)S(1)} %bitcast.88, ...), custom_call_target="tpu_custom_call" | custom-call | flops 300000000 | bytes 1000 | tf_op jit(solution)/shard_map/pallas_call | solution.py:102
  231.7 30.9 %collective-permute-done.22.refs_1_ = bf16[344,1024]{1,0:T(8,128)(2,1)S(1)} collective-permute-done((bf16[344,1024]{1,0:T(8,128)(2,1)S(1)}, bf16[344,1024]{1,0:T(8,128)(2,1)S(1)}, u32[]{:S(2)}, u32[]{:S(2)}) %collective-permute-start.22) | collective-permute-done | bytes 704544 | tf_op jit(solution)/shard_map/ppermute | solution.py:321
  262.6 5.5 %shard_map.147 = (f32[344,4096]{1,0:T(8,128)}, f32[344,4096]{1,0:T(8,128)}, f32[344,4096]{1,0:T(8,128)}, f32[344,4096]{1,0:T(8,128)}, bf16[344,1024]{1,0:T(8,128)(2,1)S(1)}) custom-call(s32[3]{0:T(128)S(1)} %pad_add_fusion.place_ref, ...), custom_call_target="tpu_custom_call", output_to_operand_aliasing={{0}: (9, {}), {1}: (10, {}), {2}: (11, {}), {3}: (12, {})} | custom-call | flops 300000000 | bytes 1000 | tf_op jit(solution)/shard_map/pallas_call | solution.py:102
  270.7 5.2 %shard_map.148 = (bf16[4,128,1024]{2,1,0:T(8,128)(2,1)S(1)}, bf16[4,128,1024]{2,1,0:T(8,128)(2,1)S(1)}, bf16[4,128,1024]{2,1,0:T(8,128)(2,1)S(1)}, bf16[4,128,1024]{2,1,0:T(8,128)(2,1)S(1)}) custom-call(s32[3]{0:T(128)S(1)} %pad_add_fusion.place_ref, bf16[512,688]{1,0:T(8,128)(2,1)S(1)} %copy.70.refs_0_, bf16[512,688]{1,0:T(8,128)(2,1)S(1)} %bitcast.89, ...), custom_call_target="tpu_custom_call" | custom-call | flops 300000000 | bytes 1000 | tf_op jit(solution)/shard_map/pallas_call | solution.py:102
  276.9 9.5 %collective-permute-done.47.refs_5_ = bf16[344,1024]{1,0:T(8,128)(2,1)S(1)} collective-permute-done((bf16[344,1024]{1,0:T(8,128)(2,1)S(1)}, bf16[344,1024]{1,0:T(8,128)(2,1)S(1)}, u32[]{:S(2)}, u32[]{:S(2)}) %collective-permute-start.47) | collective-permute-done | bytes 704544 | tf_op jit(solution)/shard_map/ppermute | solution.py:321
  286.3 5.0 %shard_map.149 = (bf16[4,128,1024]{2,1,0:T(8,128)(2,1)S(1)}, bf16[4,128,1024]{2,1,0:T(8,128)(2,1)S(1)}, bf16[4,128,1024]{2,1,0:T(8,128)(2,1)S(1)}, bf16[4,128,1024]{2,1,0:T(8,128)(2,1)S(1)}) custom-call(s32[3]{0:T(128)S(1)} %pad_add_fusion.place_ref, bf16[512,688]{1,0:T(8,128)(2,1)S(1)} %copy.70.refs_0_, bf16[512,688]{1,0:T(8,128)(2,1)S(1)} %bitcast.90, ...), custom_call_target="tpu_custom_call" | custom-call | flops 300000000 | bytes 1000 | tf_op jit(solution)/shard_map/pallas_call | solution.py:102
  294.8 2.1 collective-permute-start.39
  298.3 8.8 %collective-permute-done.34 = bf16[2,128,1024]{2,1,0:T(8,128)(2,1)S(1)} collective-permute-done((bf16[2,128,1024]{2,1,0:T(8,128)(2,1)S(1)}, bf16[2,128,1024]{2,1,0:T(8,128)(2,1)S(1)}, u32[]{:S(2)}, u32[]{:S(2)}) %collective-permute-start.34) | collective-permute-done | bytes 524320 | tf_op jit(solution)/shard_map/ppermute | solution.py:321
  307.3 11.6 %collective-permute-done.44 = bf16[4,128,1024]{2,1,0:T(8,128)(2,1)S(1)} collective-permute-done((bf16[4,128,1024]{2,1,0:T(8,128)(2,1)S(1)}, bf16[4,128,1024]{2,1,0:T(8,128)(2,1)S(1)}, u32[]{:S(2)}, u32[]{:S(2)}) %collective-permute-start.44) | collective-permute-done | bytes 1048608 | tf_op jit(solution)/shard_map/ppermute | solution.py:324
  319.3 2.1 collective-permute-start.45
  321.9 18.6 %collective-permute-done.50 = bf16[4,128,1024]{2,1,0:T(8,128)(2,1)S(1)} collective-permute-done((bf16[4,128,1024]{2,1,0:T(8,128)(2,1)S(1)}, bf16[4,128,1024]{2,1,0:T(8,128)(2,1)S(1)}, u32[]{:S(2)}, u32[]{:S(2)}) %collective-permute-start.50) | collective-permute-done | bytes 1048608 | tf_op jit(solution)/shard_map/ppermute | solution.py:324
  343.4 2.7 collective-permute-start.46
  346.1 17.9 %collective-permute-done.51 = bf16[2,128,1024]{2,1,0:T(8,128)(2,1)S(1)} collective-permute-done((bf16[2,128,1024]{2,1,0:T(8,128)(2,1)S(1)}, bf16[2,128,1024]{2,1,0:T(8,128)(2,1)S(1)}, u32[]{:S(2)}, u32[]{:S(2)}) %collective-permute-start.51) | collective-permute-done | bytes 524320 | tf_op jit(solution)/shard_map/ppermute | solution.py:321
  364.7 9.6 %collective-permute-done.46 = bf16[128,1024]{1,0:T(8,128)(2,1)S(1)} collective-permute-done((bf16[128,1024]{1,0:T(8,128)(2,1)S(1)}, bf16[128,1024]{1,0:T(8,128)(2,1)S(1)}, u32[]{:S(2)}, u32[]{:S(2)}) %collective-permute-start.46) | collective-permute-done | bytes 262176 | tf_op jit(solution)/shard_map/ppermute | solution.py:321
  374.5 4.3 %collective-permute-done.52 = bf16[128,1024]{1,0:T(8,128)(2,1)S(1)} collective-permute-done((bf16[128,1024]{1,0:T(8,128)(2,1)S(1)}, bf16[128,1024]{1,0:T(8,128)(2,1)S(1)}, u32[]{:S(2)}, u32[]{:S(2)}) %collective-permute-start.52) | collective-permute-done | bytes 262176 | tf_op jit(solution)/shard_map/ppermute | solution.py:321
  (178 shorter events, 54.5 us)
Async XLA Ops:
  10.4 11.4 %collective-permute-start.14 = (bf16[512,256]{1,0:T(8,128)(2,1)S(1)}, bf16[512,256]{1,0:T(8,128)(2,1)S(1)}, u32[]{:S(2)}, u32[]{:S(2)}) collective-permute-start(bf16[512,256]{1,0:T(8,128)(2,1)S(1)} %get-tuple-element.58), channel_id=1, source_target_pairs={{0,8},{4,12},{8,0},{12,4},{16,24},{20,28},{24,16},{28,20},{1,9},{5... | collective-permute-start | bytes 786440 | tf_op jit(solution)/shard_map/ppermute | solution.py:321
  17.4 18.9 %collective-permute-start = (bf16[688,512]{1,0:T(8,128)(2,1)}, bf16[688,512]{1,0:T(8,128)(2,1)S(1)}, u32[]{:S(2)}, u32[]{:S(2)}) collective-permute-start(bf16[688,512]{1,0:T(8,128)(2,1)} %dynamic-slice_bitcast_fusion.4), channel_id=1, source_target_pairs={{0,8},{4,12},{8,0},{12,4},{16,24},{20,28},{24,16},{28,20},{1,9},{5... | collective-permute-start | bytes 2113544 | tf_op jit(solution)/shard_map/ppermute | solution.py:321
  19.6 31.9 %collective-permute-start.1 = (bf16[688,512]{1,0:T(8,128)(2,1)}, bf16[688,512]{1,0:T(8,128)(2,1)}, u32[]{:S(2)}, u32[]{:S(2)}) collective-permute-start(bf16[688,512]{1,0:T(8,128)(2,1)} %dynamic-slice_bitcast_fusion.3), channel_id=1, source_target_pairs={{0,8},{4,12},{8,0},{12,4},{16,24},{20,28},{24,16},{28,20},{1,9},{5... | collective-permute-start | bytes 2113544 | tf_op jit(solution)/shard_map/ppermute | solution.py:321
  21.4 41.3 %collective-permute-start.10 = (bf16[512,256]{1,0:T(8,128)(2,1)}, bf16[512,256]{1,0:T(8,128)(2,1)}, u32[]{:S(2)}, u32[]{:S(2)}) collective-permute-start(bf16[512,256]{1,0:T(8,128)(2,1)} %get-tuple-element.57), channel_id=1, source_target_pairs={{0,8},{4,12},{8,0},{12,4},{16,24},{20,28},{24,16},{28,20},{1,9},{5... | collective-permute-start | bytes 786440 | tf_op jit(solution)/shard_map/ppermute | solution.py:321
  21.8 7.4 %collective-permute-start.16 = (bf16[512,256]{1,0:T(8,128)(2,1)S(1)}, bf16[512,256]{1,0:T(8,128)(2,1)}, u32[]{:S(2)}, u32[]{:S(2)}) collective-permute-start(bf16[512,256]{1,0:T(8,128)(2,1)S(1)} %collective-permute-done.14.refs_4_), channel_id=1, source_target_pairs={{0,2},{1,3},{2,0},{3,1},{4,6},{5,7},{6,4},{7,5},{8,10},{9,11},{10,... | collective-permute-start | bytes 786440 | tf_op jit(solution)/shard_map/ppermute | solution.py:324
  29.2 22.4 %collective-permute-start.17 = (bf16[512,256]{1,0:T(8,128)(2,1)}, bf16[512,256]{1,0:T(8,128)(2,1)}, u32[]{:S(2)}, u32[]{:S(2)}) collective-permute-start(bf16[512,256]{1,0:T(8,128)(2,1)} %collective-permute-done.16.refs_6_), channel_id=1, source_target_pairs={{0,1},{1,0},{2,3},{3,2},{4,5},{5,4},{6,7},{7,6},{8,9},{9,8},{10,11... | collective-permute-start | bytes 786440 | tf_op jit(solution)/shard_map/ppermute | solution.py:324
  30.0 52.2 %collective-permute-start.18 = (bf16[688,512]{1,0:T(8,128)(2,1)}, bf16[688,512]{1,0:T(8,128)(2,1)}, u32[]{:S(2)}, u32[]{:S(2)}) collective-permute-start(bf16[688,512]{1,0:T(8,128)(2,1)} %get-tuple-element.104), channel_id=1, source_target_pairs={{0,24},{4,28},{8,16},{12,20},{16,8},{20,12},{24,0},{28,4},{1,25},{... | collective-permute-start | bytes 2113544 | tf_op jit(solution)/shard_map/ppermute | solution.py:321
  61.1 58.4 %collective-permute-start.20 = (bf16[2,344,1024]{2,1,0:T(8,128)(2,1)S(1)}, bf16[2,344,1024]{2,1,0:T(8,128)(2,1)S(1)}, u32[]{:S(2)}, u32[]{:S(2)}) collective-permute-start(bf16[2,344,1024]{2,1,0:T(8,128)(2,1)S(1)} %get-tuple-element.62), channel_id=1, source_target_pairs={{0,4},{4,0},{8,12},{12,8},{16,20},{20,16},{24,28},{28,24},{1,5},{5... | collective-permute-start | bytes 4227080 | tf_op jit(solution)/shard_map/ppermute | solution.py:321
  62.7 6.6 %collective-permute-start.12 = (bf16[512,256]{1,0:T(8,128)(2,1)}, bf16[512,256]{1,0:T(8,128)(2,1)S(1)}, u32[]{:S(2)}, u32[]{:S(2)}) collective-permute-start(bf16[512,256]{1,0:T(8,128)(2,1)} %collective-permute-done.10.refs_4_), channel_id=1, source_target_pairs={{0,2},{1,3},{2,0},{3,1},{4,6},{5,7},{6,4},{7,5},{8,10},{9,11},{10,... | collective-permute-start | bytes 786440 | tf_op jit(solution)/shard_map/ppermute | solution.py:324
  64.2 14.2 %collective-permute-start.6 = (bf16[512,256]{1,0:T(8,128)(2,1)S(1)}, bf16[512,256]{1,0:T(8,128)(2,1)S(1)}, u32[]{:S(2)}, u32[]{:S(2)}) collective-permute-start(bf16[512,256]{1,0:T(8,128)(2,1)S(1)} %copy-done.26), channel_id=1, source_target_pairs={{0,8},{4,12},{8,0},{12,4},{16,24},{20,28},{24,16},{28,20},{1,9},{5... | collective-permute-start | bytes 786440 | tf_op jit(solution)/shard_map/ppermute | solution.py:321
  65.6 14.5 %collective-permute-start.11 = (bf16[512,256]{1,0:T(8,128)(2,1)}, bf16[512,256]{1,0:T(8,128)(2,1)S(1)}, u32[]{:S(2)}, u32[]{:S(2)}) collective-permute-start(bf16[512,256]{1,0:T(8,128)(2,1)} %collective-permute-done.10.refs_4_), channel_id=1, source_target_pairs={{0,1},{1,0},{2,3},{3,2},{4,5},{5,4},{6,7},{7,6},{8,9},{9,8},{10,11... | collective-permute-start | bytes 786440 | tf_op jit(solution)/shard_map/ppermute | solution.py:324
  69.3 13.4 %collective-permute-start.13 = (bf16[512,256]{1,0:T(8,128)(2,1)S(1)}, bf16[512,256]{1,0:T(8,128)(2,1)S(1)}, u32[]{:S(2)}, u32[]{:S(2)}) collective-permute-start(bf16[512,256]{1,0:T(8,128)(2,1)S(1)} %collective-permute-done.12.refs_6_), channel_id=1, source_target_pairs={{0,1},{1,0},{2,3},{3,2},{4,5},{5,4},{6,7},{7,6},{8,9},{9,8},{10,11... | collective-permute-start | bytes 786440 | tf_op jit(solution)/shard_map/ppermute | solution.py:324
  78.5 33.4 %collective-permute-start.19 = (bf16[688,512]{1,0:T(8,128)(2,1)S(1)}, bf16[688,512]{1,0:T(8,128)(2,1)S(1)}, u32[]{:S(2)}, u32[]{:S(2)}) collective-permute-start(bf16[688,512]{1,0:T(8,128)(2,1)S(1)} %copy-done.28), channel_id=1, source_target_pairs={{0,16},{4,20},{8,24},{12,28},{16,0},{20,4},{24,8},{28,12},{1,17},{... | collective-permute-start | bytes 2113544 | tf_op jit(solution)/shard_map/ppermute | solution.py:321
  80.1 19.5 %collective-permute-start.2 = (bf16[512,256]{1,0:T(8,128)(2,1)S(1)}, bf16[512,256]{1,0:T(8,128)(2,1)}, u32[]{:S(2)}, u32[]{:S(2)}) collective-permute-start(bf16[512,256]{1,0:T(8,128)(2,1)S(1)} %copy-done.24), channel_id=1, source_target_pairs={{0,8},{4,12},{8,0},{12,4},{16,24},{20,28},{24,16},{28,20},{1,9},{5... | collective-permute-start | bytes 786440 | tf_op jit(solution)/shard_map/ppermute | solution.py:321
  82.2 17.5 %collective-permute-start.8 = (bf16[512,256]{1,0:T(8,128)(2,1)S(1)}, bf16[512,256]{1,0:T(8,128)(2,1)S(1)}, u32[]{:S(2)}, u32[]{:S(2)}) collective-permute-start(bf16[512,256]{1,0:T(8,128)(2,1)S(1)} %collective-permute-done.6.refs_4_), channel_id=1, source_target_pairs={{0,2},{1,3},{2,0},{3,1},{4,6},{5,7},{6,4},{7,5},{8,10},{9,11},{10,... | collective-permute-start | bytes 786440 | tf_op jit(solution)/shard_map/ppermute | solution.py:324
  88.9 46.9 %collective-permute-start.25 = (bf16[2,344,1024]{2,1,0:T(8,128)(2,1)}, bf16[2,344,1024]{2,1,0:T(8,128)(2,1)}, u32[]{:S(2)}, u32[]{:S(2)}) collective-permute-start(bf16[2,344,1024]{2,1,0:T(8,128)(2,1)} %get-tuple-element.66), channel_id=1, source_target_pairs={{0,4},{4,0},{8,12},{12,8},{16,20},{20,16},{24,28},{28,24},{1,5},{5... | collective-permute-start | bytes 4227080 | tf_op jit(solution)/shard_map/ppermute | solution.py:321
  99.6 12.2 %collective-permute-start.9 = (bf16[512,256]{1,0:T(8,128)(2,1)S(1)}, bf16[512,256]{1,0:T(8,128)(2,1)S(1)}, u32[]{:S(2)}, u32[]{:S(2)}) collective-permute-start(bf16[512,256]{1,0:T(8,128)(2,1)S(1)} %collective-permute-done.8.refs_6_), channel_id=1, source_target_pairs={{0,1},{1,0},{2,3},{3,2},{4,5},{5,4},{6,7},{7,6},{8,9},{9,8},{10,11... | collective-permute-start | bytes 786440 | tf_op jit(solution)/shard_map/ppermute | solution.py:324
  101.2 20.2 %collective-permute-start.4 = (bf16[512,256]{1,0:T(8,128)(2,1)}, bf16[512,256]{1,0:T(8,128)(2,1)}, u32[]{:S(2)}, u32[]{:S(2)}) collective-permute-start(bf16[512,256]{1,0:T(8,128)(2,1)} %collective-permute-done.2.refs_4_), channel_id=1, source_target_pairs={{0,2},{1,3},{2,0},{3,1},{4,6},{5,7},{6,4},{7,5},{8,10},{9,11},{10,... | collective-permute-start | bytes 786440 | tf_op jit(solution)/shard_map/ppermute | solution.py:324
  118.0 43.2 %collective-permute-start.23 = (bf16[2,344,1024]{2,1,0:T(8,128)(2,1)}, bf16[2,344,1024]{2,1,0:T(8,128)(2,1)}, u32[]{:S(2)}, u32[]{:S(2)}) collective-permute-start(bf16[2,344,1024]{2,1,0:T(8,128)(2,1)} %get-tuple-element.65), channel_id=1, source_target_pairs={{0,4},{4,0},{8,12},{12,8},{16,20},{20,16},{24,28},{28,24},{1,5},{5... | collective-permute-start | bytes 4227080 | tf_op jit(solution)/shard_map/ppermute | solution.py:321
  121.3 33.6 %collective-permute-start.27 = (bf16[344,1024]{1,0:T(8,128)(2,1)}, bf16[344,1024]{1,0:T(8,128)(2,1)}, u32[]{:S(2)}, u32[]{:S(2)}) collective-permute-start(bf16[344,1024]{1,0:T(8,128)(2,1)} %get-tuple-element.108.refs_10_), channel_id=1, source_target_pairs={{0,16},{4,20},{8,24},{12,28},{16,0},{20,4},{24,8},{28,12},{1,17},{... | collective-permute-start | bytes 2113544 | tf_op jit(solution)/shard_map/ppermute | solution.py:321
  123.2 44.1 %collective-permute-start.28 = (bf16[688,512]{1,0:T(8,128)(2,1)}, bf16[688,512]{1,0:T(8,128)(2,1)}, u32[]{:S(2)}, u32[]{:S(2)}) collective-permute-start(bf16[688,512]{1,0:T(8,128)(2,1)} %get-tuple-element.103), channel_id=1, source_target_pairs={{0,8},{4,12},{8,0},{12,4},{16,24},{20,28},{24,16},{28,20},{1,9},{5... | collective-permute-start | bytes 2113544 | tf_op jit(solution)/shard_map/ppermute | solution.py:321
  135.2 77.3 %collective-permute-start.21 = (bf16[2,344,1024]{2,1,0:T(8,128)(2,1)}, bf16[2,344,1024]{2,1,0:T(8,128)(2,1)}, u32[]{:S(2)}, u32[]{:S(2)}) collective-permute-start(bf16[2,344,1024]{2,1,0:T(8,128)(2,1)} %get-tuple-element.64), channel_id=1, source_target_pairs={{0,4},{4,0},{8,12},{12,8},{16,20},{20,16},{24,28},{28,24},{1,5},{5... | collective-permute-start | bytes 4227080 | tf_op jit(solution)/shard_map/ppermute | solution.py:321
  139.0 60.3 %collective-permute-start.26 = (bf16[344,1024]{1,0:T(8,128)(2,1)}, bf16[344,1024]{1,0:T(8,128)(2,1)}, u32[]{:S(2)}, u32[]{:S(2)}) collective-permute-start(bf16[344,1024]{1,0:T(8,128)(2,1)} %get-tuple-element.109.refs_9_), channel_id=1, source_target_pairs={{0,16},{4,20},{8,24},{12,28},{16,0},{20,4},{24,8},{28,12},{1,17},{... | collective-permute-start | bytes 2113544 | tf_op jit(solution)/shard_map/ppermute | solution.py:321
  160.7 45.7 %collective-permute-start.29 = (bf16[344,1024]{1,0:T(8,128)(2,1)}, bf16[344,1024]{1,0:T(8,128)(2,1)}, u32[]{:S(2)}, u32[]{:S(2)}) collective-permute-start(bf16[344,1024]{1,0:T(8,128)(2,1)} %get-tuple-element.71.refs_12_.refs_4_), channel_id=1, source_target_pairs={{0,4},{4,0},{8,12},{12,8},{16,20},{20,16},{24,28},{28,24},{1,5},{5... | collective-permute-start | bytes 2113544 | tf_op jit(solution)/shard_map/ppermute | solution.py:321
  164.3 50.3 %collective-permute-start.24 = (bf16[344,1024]{1,0:T(8,128)(2,1)}, bf16[344,1024]{1,0:T(8,128)(2,1)}, u32[]{:S(2)}, u32[]{:S(2)}) collective-permute-start(bf16[344,1024]{1,0:T(8,128)(2,1)} %get-tuple-element.111.refs_7_), channel_id=1, source_target_pairs={{0,16},{4,20},{8,24},{12,28},{16,0},{20,4},{24,8},{28,12},{1,17},{... | collective-permute-start | bytes 2113544 | tf_op jit(solution)/shard_map/ppermute | solution.py:321
  206.0 17.6 %collective-permute-start.30 = (bf16[344,1024]{1,0:T(8,128)(2,1)S(1)}, bf16[344,1024]{1,0:T(8,128)(2,1)S(1)}, u32[]{:S(2)}, u32[]{:S(2)}) collective-permute-start(bf16[344,1024]{1,0:T(8,128)(2,1)S(1)} %get-tuple-element.76.refs_6_.refs_4_), channel_id=1, source_target_pairs={{0,4},{4,0},{8,12},{12,8},{16,20},{20,16},{24,28},{28,24},{1,5},{5... | collective-permute-start | bytes 2113544 | tf_op jit(solution)/shard_map/ppermute | solution.py:321
  212.5 16.7 %collective-permute-start.31 = (bf16[4,128,1024]{2,1,0:T(8,128)(2,1)S(1)}, bf16[4,128,1024]{2,1,0:T(8,128)(2,1)S(1)}, u32[]{:S(2)}, u32[]{:S(2)}) collective-permute-start(bf16[4,128,1024]{2,1,0:T(8,128)(2,1)S(1)} %get-tuple-element.85), channel_id=1, source_target_pairs={{0,1},{1,0},{2,3},{3,2},{4,5},{5,4},{6,7},{7,6},{8,9},{9,8},{10,11... | collective-permute-start | bytes 3145736 | tf_op jit(solution)/shard_map/ppermute | solution.py:324
  228.5 39.6 %collective-permute-start.37 = (bf16[4,128,1024]{2,1,0:T(8,128)(2,1)S(1)}, bf16[4,128,1024]{2,1,0:T(8,128)(2,1)S(1)}, u32[]{:S(2)}, u32[]{:S(2)}) collective-permute-start(bf16[4,128,1024]{2,1,0:T(8,128)(2,1)S(1)} %get-tuple-element.93), channel_id=1, source_target_pairs={{0,1},{1,0},{2,3},{3,2},{4,5},{5,4},{6,7},{7,6},{8,9},{9,8},{10,11... | collective-permute-start | bytes 3145736 | tf_op jit(solution)/shard_map/ppermute | solution.py:324
  228.6 33.9 %collective-permute-start.22 = (bf16[344,1024]{1,0:T(8,128)(2,1)S(1)}, bf16[344,1024]{1,0:T(8,128)(2,1)S(1)}, u32[]{:S(2)}, u32[]{:S(2)}) collective-permute-start(bf16[344,1024]{1,0:T(8,128)(2,1)S(1)} %get-tuple-element.113.refs_13_), channel_id=1, source_target_pairs={{0,16},{4,20},{8,24},{12,28},{16,0},{20,4},{24,8},{28,12},{1,17},{... | collective-permute-start | bytes 2113544 | tf_op jit(solution)/shard_map/ppermute | solution.py:321
  228.7 47.2 %collective-permute-start.32 = (bf16[4,128,1024]{2,1,0:T(8,128)(2,1)S(1)}, bf16[4,128,1024]{2,1,0:T(8,128)(2,1)S(1)}, u32[]{:S(2)}, u32[]{:S(2)}) collective-permute-start(bf16[4,128,1024]{2,1,0:T(8,128)(2,1)S(1)} %get-tuple-element.90), channel_id=1, source_target_pairs={{0,1},{1,0},{2,3},{3,2},{4,5},{5,4},{6,7},{7,6},{8,9},{9,8},{10,11... | collective-permute-start | bytes 3145736 | tf_op jit(solution)/shard_map/ppermute | solution.py:324
  229.6 46.9 %collective-permute-start.33 = (bf16[4,128,1024]{2,1,0:T(8,128)(2,1)S(1)}, bf16[4,128,1024]{2,1,0:T(8,128)(2,1)S(1)}, u32[]{:S(2)}, u32[]{:S(2)}) collective-permute-start(bf16[4,128,1024]{2,1,0:T(8,128)(2,1)S(1)} %add_convert_fusion.7.refs_13_), channel_id=1, source_target_pairs={{0,2},{1,3},{2,0},{3,1},{4,6},{5,7},{6,4},{7,5},{8,10},{9,11},{10,... | collective-permute-start | bytes 3145736 | tf_op jit(solution)/shard_map/ppermute | solution.py:324
  231.2 38.0 %collective-permute-start.41 = (bf16[344,1024]{1,0:T(8,128)(2,1)S(1)}, bf16[344,1024]{1,0:T(8,128)(2,1)S(1)}, u32[]{:S(2)}, u32[]{:S(2)}) collective-permute-start(bf16[344,1024]{1,0:T(8,128)(2,1)S(1)} %get-tuple-element.82.refs_6_.refs_4_), channel_id=1, source_target_pairs={{0,4},{4,0},{8,12},{12,8},{16,20},{20,16},{24,28},{28,24},{1,5},{5... | collective-permute-start | bytes 2113544 | tf_op jit(solution)/shard_map/ppermute | solution.py:321
  262.5 29.3 %collective-permute-start.36 = (bf16[4,128,1024]{2,1,0:T(8,128)(2,1)S(1)}, bf16[4,128,1024]{2,1,0:T(8,128)(2,1)S(1)}, u32[]{:S(2)}, u32[]{:S(2)}) collective-permute-start(bf16[4,128,1024]{2,1,0:T(8,128)(2,1)S(1)} %get-tuple-element.91), channel_id=1, source_target_pairs={{0,1},{1,0},{2,3},{3,2},{4,5},{5,4},{6,7},{7,6},{8,9},{9,8},{10,11... | collective-permute-start | bytes 3145736 | tf_op jit(solution)/shard_map/ppermute | solution.py:324
  268.1 18.2 %collective-permute-start.47 = (bf16[344,1024]{1,0:T(8,128)(2,1)S(1)}, bf16[344,1024]{1,0:T(8,128)(2,1)S(1)}, u32[]{:S(2)}, u32[]{:S(2)}) collective-permute-start(bf16[344,1024]{1,0:T(8,128)(2,1)S(1)} %get-tuple-element.94.refs_6_.refs_4_), channel_id=1, source_target_pairs={{0,4},{4,0},{8,12},{12,8},{16,20},{20,16},{24,28},{28,24},{1,5},{5... | collective-permute-start | bytes 2113544 | tf_op jit(solution)/shard_map/ppermute | solution.py:321
  269.1 25.3 %collective-permute-start.38 = (bf16[4,128,1024]{2,1,0:T(8,128)(2,1)S(1)}, bf16[4,128,1024]{2,1,0:T(8,128)(2,1)S(1)}, u32[]{:S(2)}, u32[]{:S(2)}) collective-permute-start(bf16[4,128,1024]{2,1,0:T(8,128)(2,1)S(1)} %add_convert_fusion.4.refs_7_), channel_id=1, source_target_pairs={{0,2},{1,3},{2,0},{3,1},{4,6},{5,7},{6,4},{7,5},{8,10},{9,11},{10,... | collective-permute-start | bytes 3145736 | tf_op jit(solution)/shard_map/ppermute | solution.py:324
  275.9 16.5 %collective-permute-start.43 = (bf16[4,128,1024]{2,1,0:T(8,128)(2,1)S(1)}, bf16[4,128,1024]{2,1,0:T(8,128)(2,1)S(1)}, u32[]{:S(2)}, u32[]{:S(2)}) collective-permute-start(bf16[4,128,1024]{2,1,0:T(8,128)(2,1)S(1)} %get-tuple-element.98), channel_id=1, source_target_pairs={{0,1},{1,0},{2,3},{3,2},{4,5},{5,4},{6,7},{7,6},{8,9},{9,8},{10,11... | collective-permute-start | bytes 3145736 | tf_op jit(solution)/shard_map/ppermute | solution.py:324
  291.4 5.9 %collective-permute-start.42 = (bf16[4,128,1024]{2,1,0:T(8,128)(2,1)S(1)}, bf16[4,128,1024]{2,1,0:T(8,128)(2,1)S(1)}, u32[]{:S(2)}, u32[]{:S(2)}) collective-permute-start(bf16[4,128,1024]{2,1,0:T(8,128)(2,1)S(1)} %get-tuple-element.96), channel_id=1, source_target_pairs={{0,1},{1,0},{2,3},{3,2},{4,5},{5,4},{6,7},{7,6},{8,9},{9,8},{10,11... | collective-permute-start | bytes 3145736 | tf_op jit(solution)/shard_map/ppermute | solution.py:324
  292.3 14.8 %collective-permute-start.34 = (bf16[2,128,1024]{2,1,0:T(8,128)(2,1)S(1)}, bf16[2,128,1024]{2,1,0:T(8,128)(2,1)S(1)}, u32[]{:S(2)}, u32[]{:S(2)}) collective-permute-start(bf16[2,128,1024]{2,1,0:T(8,128)(2,1)S(1)} %get-tuple-element.118.refs_8_), channel_id=1, source_target_pairs={{0,8},{4,12},{8,0},{12,4},{16,24},{20,28},{24,16},{28,20},{1,9},{5... | collective-permute-start | bytes 1572872 | tf_op jit(solution)/shard_map/ppermute | solution.py:321
  292.8 26.1 %collective-permute-start.44 = (bf16[4,128,1024]{2,1,0:T(8,128)(2,1)S(1)}, bf16[4,128,1024]{2,1,0:T(8,128)(2,1)S(1)}, u32[]{:S(2)}, u32[]{:S(2)}) collective-permute-start(bf16[4,128,1024]{2,1,0:T(8,128)(2,1)S(1)} %add_convert_fusion.2), channel_id=1, source_target_pairs={{0,2},{1,3},{2,0},{3,1},{4,6},{5,7},{6,4},{7,5},{8,10},{9,11},{10,... | collective-permute-start | bytes 3145736 | tf_op jit(solution)/shard_map/ppermute | solution.py:324
  294.8 47.9 %collective-permute-start.39 = (bf16[2,128,1024]{2,1,0:T(8,128)(2,1)S(1)}, bf16[2,128,1024]{2,1,0:T(8,128)(2,1)S(1)}, u32[]{:S(2)}, u32[]{:S(2)}) collective-permute-start(bf16[2,128,1024]{2,1,0:T(8,128)(2,1)S(1)} %get-tuple-element.120), channel_id=1, source_target_pairs={{0,8},{4,12},{8,0},{12,4},{16,24},{20,28},{24,16},{28,20},{1,9},{5... | collective-permute-start | bytes 1572872 | tf_op jit(solution)/shard_map/ppermute | solution.py:321
  296.9 24.5 %collective-permute-start.48 = (bf16[4,128,1024]{2,1,0:T(8,128)(2,1)S(1)}, bf16[4,128,1024]{2,1,0:T(8,128)(2,1)S(1)}, u32[]{:S(2)}, u32[]{:S(2)}) collective-permute-start(bf16[4,128,1024]{2,1,0:T(8,128)(2,1)S(1)} %get-tuple-element.100), channel_id=1, source_target_pairs={{0,1},{1,0},{2,3},{3,2},{4,5},{5,4},{6,7},{7,6},{8,9},{9,8},{10,11... | collective-permute-start | bytes 3145736 | tf_op jit(solution)/shard_map/ppermute | solution.py:324
  297.3 43.2 %collective-permute-start.50 = (bf16[4,128,1024]{2,1,0:T(8,128)(2,1)S(1)}, bf16[4,128,1024]{2,1,0:T(8,128)(2,1)S(1)}, u32[]{:S(2)}, u32[]{:S(2)}) collective-permute-start(bf16[4,128,1024]{2,1,0:T(8,128)(2,1)S(1)} %add_convert_fusion), channel_id=1, source_target_pairs={{0,2},{1,3},{2,0},{3,1},{4,6},{5,7},{6,4},{7,5},{8,10},{9,11},{10,... | collective-permute-start | bytes 3145736 | tf_op jit(solution)/shard_map/ppermute | solution.py:324
  307.2 35.9 %collective-permute-start.35 = (bf16[128,1024]{1,0:T(8,128)(2,1)S(1)}, bf16[128,1024]{1,0:T(8,128)(2,1)S(1)}, u32[]{:S(2)}, u32[]{:S(2)}) collective-permute-start(bf16[128,1024]{1,0:T(8,128)(2,1)S(1)} %fusion.13), channel_id=1, source_target_pairs={{0,16},{4,20},{8,24},{12,28},{16,0},{20,4},{24,8},{28,12},{1,17},{... | collective-permute-start | bytes 786440 | tf_op jit(solution)/shard_map/ppermute | solution.py:321
  319.3 23.9 %collective-permute-start.45 = (bf16[2,128,1024]{2,1,0:T(8,128)(2,1)S(1)}, bf16[2,128,1024]{2,1,0:T(8,128)(2,1)S(1)}, u32[]{:S(2)}, u32[]{:S(2)}) collective-permute-start(bf16[2,128,1024]{2,1,0:T(8,128)(2,1)S(1)} %get-tuple-element.122), channel_id=1, source_target_pairs={{0,8},{4,12},{8,0},{12,4},{16,24},{20,28},{24,16},{28,20},{1,9},{5... | collective-permute-start | bytes 1572872 | tf_op jit(solution)/shard_map/ppermute | solution.py:321
  340.9 23.1 %collective-permute-start.51 = (bf16[2,128,1024]{2,1,0:T(8,128)(2,1)S(1)}, bf16[2,128,1024]{2,1,0:T(8,128)(2,1)S(1)}, u32[]{:S(2)}, u32[]{:S(2)}) collective-permute-start(bf16[2,128,1024]{2,1,0:T(8,128)(2,1)S(1)} %get-tuple-element.124), channel_id=1, source_target_pairs={{0,8},{4,12},{8,0},{12,4},{16,24},{20,28},{24,16},{28,20},{1,9},{5... | collective-permute-start | bytes 1572872 | tf_op jit(solution)/shard_map/ppermute | solution.py:321
  342.8 21.8 %collective-permute-start.40 = (bf16[128,1024]{1,0:T(8,128)(2,1)S(1)}, bf16[128,1024]{1,0:T(8,128)(2,1)S(1)}, u32[]{:S(2)}, u32[]{:S(2)}) collective-permute-start(bf16[128,1024]{1,0:T(8,128)(2,1)S(1)} %fusion.15), channel_id=1, source_target_pairs={{0,16},{4,20},{8,24},{12,28},{16,0},{20,4},{24,8},{28,12},{1,17},{... | collective-permute-start | bytes 786440 | tf_op jit(solution)/shard_map/ppermute | solution.py:321
  343.4 31.0 %collective-permute-start.46 = (bf16[128,1024]{1,0:T(8,128)(2,1)S(1)}, bf16[128,1024]{1,0:T(8,128)(2,1)S(1)}, u32[]{:S(2)}, u32[]{:S(2)}) collective-permute-start(bf16[128,1024]{1,0:T(8,128)(2,1)S(1)} %fusion.17), channel_id=1, source_target_pairs={{0,16},{4,20},{8,24},{12,28},{16,0},{20,4},{24,8},{28,12},{1,17},{... | collective-permute-start | bytes 786440 | tf_op jit(solution)/shard_map/ppermute | solution.py:321
  364.1 14.7 %collective-permute-start.52 = (bf16[128,1024]{1,0:T(8,128)(2,1)S(1)}, bf16[128,1024]{1,0:T(8,128)(2,1)S(1)}, u32[]{:S(2)}, u32[]{:S(2)}) collective-permute-start(bf16[128,1024]{1,0:T(8,128)(2,1)S(1)} %fusion.19), channel_id=1, source_target_pairs={{0,16},{4,20},{8,24},{12,28},{16,0},{20,4},{24,8},{28,12},{1,17},{... | collective-permute-start | bytes 786440 | tf_op jit(solution)/shard_map/ppermute | solution.py:321
  (37 other events, 317.2 us)
